TPU v7x, 256 devices: a whole 4x4x8 slice. The times are simulated.
256 devices in a mesh: dp: 16 (over z_lo, y), expert: 16 (over x, z_hi, core).
Axes of the slice: x: 4, y: 4, z: 8 (z_hi: 2, z_lo: 4; z = z_hi * 4 + z_lo), core: 2. Of those that a mesh axis runs over, the one named last changes fastest.
Arguments:
- values: bfloat16 [2048, 3072], P('expert', 'dp'), may hold values from -6 to 6
- exponents: int32 [2048, 24], P('expert'), may hold values from -2 to 2
- expert_ids: int32 [2048, 4], P('expert'), may hold values from 0 to 15, all different within a row; in each aligned block of 128 rows (0 to 127, 128 to 255, ...) at most 36 rows name the same one
- route_weights: bfloat16 [2048, 4], P('expert'), may hold values from 0.049804688 to 0.59765625
- cotangent: bfloat16 [2048, 3072], P('expert', 'dp'), may hold values from -2 to 2
- w_gate: bfloat16 [16, 5376, 3072], P('expert', 'dp'), may hold values from -0.109375 to 0.109375
- w_up: bfloat16 [16, 5376, 3072], P('expert', 'dp'), may hold values from -0.109375 to 0.109375
- w_down: bfloat16 [16, 5376, 3072], P('expert', 'dp'), may hold values from -0.078125 to 0.078125
Outputs:
- d_values: bfloat16 [2048, 3072], P('expert', 'dp')
- d_route_weights: bfloat16 [2048, 4], P('expert')
- grad_gate: bfloat16 [16, 5376, 3072], P('expert', 'dp')
- grad_up: bfloat16 [16, 5376, 3072], P('expert', 'dp')
- grad_down: bfloat16 [16, 5376, 3072], P('expert', 'dp')
Inputs may be any that keep to these rules, and one draw needn't show every extreme that they name: `expert_ids`: each row names 4 different experts. Among the rows of one index of expert no expert is named more than 36 times, a bound that some block reaches.
All inputs are finite; a program needn't handle non-finite values.
Results may differ from a plain program's by a relative error of at most 0.024.
Values may be sent and summed in bfloat16 or wider, within the bound.
A program may use at most 128 MiB of HBM per device.

v0:
```python
import jax
import jax.numpy as jnp
from jax import lax
from jax.sharding import PartitionSpec as P


def contract(left, right, left_dim, right_dim):
    return lax.dot_general(
        left, right, (((left_dim,), (right_dim,)), ((), ())), preferred_element_type=jnp.float32
    )


def dequantize(rows, scales_in):
    count, width = rows.shape
    blocks = scales_in.shape[1]
    factor = jnp.exp2(scales_in.astype(jnp.float32))
    return (
        (rows.astype(jnp.float32).reshape(count, blocks, width // blocks) * factor[:, :, None])
        .reshape(count, width)
        .astype(jnp.bfloat16)
    )


def forward_rows(inputs, gate_w, up_w, down_w):
    gate = contract(inputs, gate_w, 1, 1)
    upper = contract(inputs, up_w, 1, 1)
    sigmoid_gate = jax.nn.sigmoid(gate)
    swished = gate * sigmoid_gate
    hidden = (swished * upper).astype(jnp.bfloat16)
    output = jnp.dot(hidden, down_w, preferred_element_type=jnp.float32)
    return (gate, upper, sigmoid_gate, swished, hidden, output)


def backward_rows(inputs, saved, out_cot, probs, gate_w, up_w, down_w):
    gate, upper, sigmoid_gate, swished, hidden, output = saved
    prob_part = jnp.sum(output * out_cot.astype(jnp.float32), axis=1)
    scaled_cot = (probs.astype(jnp.float32)[:, None] * out_cot.astype(jnp.float32)).astype(
        jnp.bfloat16
    )
    hidden_grad = contract(scaled_cot, down_w, 1, 1)
    gate_grad = (hidden_grad * upper * sigmoid_gate * (1.0 + gate * (1.0 - sigmoid_gate))).astype(
        jnp.bfloat16
    )
    upper_grad = (hidden_grad * swished).astype(jnp.bfloat16)
    input_part = jnp.dot(gate_grad, gate_w, preferred_element_type=jnp.float32) + jnp.dot(
        upper_grad, up_w, preferred_element_type=jnp.float32
    )
    weight_gate = contract(gate_grad, inputs, 0, 0)
    weight_up = contract(upper_grad, inputs, 0, 0)
    weight_down = contract(hidden, scaled_cot, 0, 0)
    return (input_part, prob_part, weight_gate, weight_up, weight_down)


def on_device(values, exponents, expert_ids, route_weights, cotangent, w_gate, w_up, w_down):
    rows_full, cot_full = (
        lax.all_gather(values, "dp", axis=1, tiled=True),
        lax.all_gather(cotangent, "dp", axis=1, tiled=True),
    )
    tok_rows, width = rows_full.shape
    share = values.shape[1]
    blocks = exponents.shape[1]
    top_count = expert_ids.shape[1]
    groups = lax.axis_size("expert")
    local_count = w_gate.shape[0]
    total_experts = groups * local_count
    capacity = min(tok_rows, 9 * tok_rows * top_count // (8 * total_experts))
    slot_count = total_experts * capacity
    onehot = (expert_ids[:, :, None] == jnp.arange(total_experts, dtype=jnp.int32)).astype(
        jnp.int32
    )
    flat_hot = onehot.reshape(tok_rows * top_count, total_experts)
    before = jnp.cumsum(flat_hot, axis=0) - flat_hot
    position = jnp.sum(flat_hot * before, axis=1).reshape(tok_rows, top_count)
    target = expert_ids * capacity + position
    hits = target[None, :, :] == jnp.arange(slot_count, dtype=jnp.int32)[:, None, None]
    picker = jnp.any(hits, axis=2).astype(jnp.bfloat16)
    send_values = jnp.dot(picker, rows_full, preferred_element_type=jnp.float32).astype(
        jnp.bfloat16
    )
    send_scales = jnp.dot(
        picker, exponents.astype(jnp.bfloat16), preferred_element_type=jnp.float32
    ).astype(jnp.bfloat16)
    send_cot = jnp.dot(picker, cot_full, preferred_element_type=jnp.float32).astype(jnp.bfloat16)
    send_prob = jnp.sum(
        jnp.where(hits, route_weights.astype(jnp.float32)[None], 0.0), axis=(1, 2)
    ).astype(jnp.bfloat16)
    slab = local_count * capacity
    send_values = send_values.reshape(groups, slab, width)
    send_scales = send_scales.reshape(groups, slab, blocks)
    send_cot = send_cot.reshape(groups, slab, width)
    send_prob = send_prob.reshape(groups, slab)
    recv_values, recv_scales = (
        lax.all_to_all(send_values, "expert", split_axis=0, concat_axis=0, tiled=True),
        lax.all_to_all(send_scales, "expert", split_axis=0, concat_axis=0, tiled=True),
    )

    def local_rows(array, local):
        piece = array.reshape((groups, local_count, capacity) + array.shape[2:])[:, local]
        return piece.reshape((groups * capacity,) + array.shape[2:])

    local = 0
    inputs = dequantize(local_rows(recv_values, local), local_rows(recv_scales, local))
    inputs_list = [inputs]
    saved_list = [forward_rows(inputs, w_gate[local], w_up[local], w_down[local])]
    recv_cot, recv_prob = (
        lax.all_to_all(send_cot, "expert", split_axis=0, concat_axis=0, tiled=True),
        lax.all_to_all(send_prob, "expert", split_axis=0, concat_axis=0, tiled=True),
    )
    local = 0
    results = backward_rows(
        inputs_list[local],
        saved_list[local],
        local_rows(recv_cot, local),
        local_rows(recv_prob, local),
        w_gate[local],
        w_up[local],
        w_down[local],
    )
    input_parts = results[0].reshape(groups, 1, capacity, width)
    prob_parts = results[1].reshape(groups, 1, capacity)
    gate_parts = [results[2].astype(jnp.bfloat16)]
    upper_parts = [results[3].astype(jnp.bfloat16)]
    down_parts = [results[4].astype(jnp.bfloat16)]
    part_rows = input_parts.reshape(groups, slab, width)
    part_prob = prob_parts.reshape(groups, slab)
    total_prob = lax.psum(part_prob, "dp").astype(jnp.bfloat16)
    summed_rows = lax.psum_scatter(
        part_rows.astype(jnp.bfloat16), "dp", scatter_dimension=2, tiled=True
    )
    back_rows, back_prob = (
        lax.all_to_all(summed_rows, "expert", split_axis=0, concat_axis=0, tiled=True),
        lax.all_to_all(total_prob, "expert", split_axis=0, concat_axis=0, tiled=True),
    )
    back_rows = back_rows.reshape(slot_count, share)
    back_prob = back_prob.reshape(slot_count).astype(jnp.float32)
    summed = contract(picker, back_rows, 0, 0)
    offset = lax.axis_index("dp") * share
    columns = offset + jnp.arange(share, dtype=jnp.int32)
    block_map = ((columns // 128)[None, :] == jnp.arange(blocks, dtype=jnp.int32)[:, None]).astype(
        jnp.float32
    )
    factor_cols = jnp.dot(
        jnp.exp2(exponents.astype(jnp.float32)), block_map, precision=lax.Precision.HIGHEST
    )
    d_values = (summed * factor_cols).astype(jnp.bfloat16)
    d_route = jnp.sum(jnp.where(hits, back_prob[:, None, None], 0.0), axis=0).astype(jnp.bfloat16)
    return (d_values, d_route, jnp.stack(gate_parts), jnp.stack(upper_parts), jnp.stack(down_parts))


def solution(mesh):
    in_specs = (
        P("expert", "dp"),
        P("expert", None),
        P("expert", None),
        P("expert", None),
        P("expert", "dp"),
        P("expert", "dp", None),
        P("expert", "dp", None),
        P("expert", "dp", None),
    )
    out_specs = (
        P("expert", "dp"),
        P("expert", None),
        P("expert", "dp", None),
        P("expert", "dp", None),
        P("expert", "dp", None),
    )
    return jax.shard_map(
        on_device, mesh=mesh, in_specs=in_specs, out_specs=out_specs, check_vma=False
    )
```

profile of v0, /device:TPU:1, one launch (start us, length us, event | category | flops | bytes accessed | tf_op | source)
XLA Modules:
  0.0 565.3 jit_solution(9589954215481868224)
XLA Ops:
  7.2 0.9 copy.52
  8.3 1.2 reduce-window.6
  10.0 0.7 multiply_add_fusion
  10.9 0.9 convolution_convert_fusion.5
  12.0 0.8 reshape.179
  12.8 12.4 %all-to-all-start.3 = ((bf16[16,2,432]{2,1,0:T(2,128)(2,1)}), bf16[16,2,432]{2,1,0:T(2,128)(2,1)S(1)}, u32[]{:S(2)}, u32[]{:S(2)}) async-start(bf16[16,2,432]{2,1,0:T(2,128)(2,1)} %reshape.179), calls=%async_computation.3 | async-start | bytes 65536 | tf_op jit(solution)/shard_map/all_to_all | solution.py:94
  25.2 39.0 %all_gather.7 = bf16[128,3072]{0,1:T(8,128)(2,1)S(1)} all-gather(bf16[128,192]{0,1:T(8,128)(2,1)} %param.8), channel_id=1, replica_groups=mesh['dp'=16,'expert'=16] {'dp'}, dimensions={1}, use_global_device_ids=true | all-gather | bytes 835584 | tf_op jit(solution)/shard_map/all_gather | solution.py:56
  64.2 2.8 convolution_convert_fusion
  67.1 4.7 reshape.155
  71.8 16.6 %all-to-all-start.2 = ((bf16[16,36,3072]{2,1,0:T(8,128)(2,1)}), bf16[16,36,3072]{2,1,0:T(8,128)(2,1)}, u32[]{:S(2)}, u32[]{:S(2)}) async-start(bf16[16,36,3072]{2,1,0:T(8,128)(2,1)} %reshape.155), calls=%async_computation.2 | async-start | bytes 7864320 | tf_op jit(solution)/shard_map/all_to_all | solution.py:93
  88.5 116.6 %all_gather.6 = bf16[128,3072]{0,1:T(8,128)(2,1)S(1)} all-gather(bf16[128,192]{0,1:T(8,128)(2,1)S(1)} %copy-done.9), channel_id=1, replica_groups=mesh['dp'=16,'expert'=16] {'dp'}, dimensions={1}, use_global_device_ids=true | all-gather | bytes 835584 | tf_op jit(solution)/shard_map/all_gather | solution.py:57
  205.0 2.8 convolution_convert_fusion.1
  207.9 4.7 reshape.154
  212.5 11.1 %all-to-all-start.1 = ((bf16[16,36,3072]{2,1,0:T(8,128)(2,1)}), bf16[16,36,3072]{2,1,0:T(8,128)(2,1)}, u32[]{:S(2)}, u32[]{:S(2)}) async-start(bf16[16,36,3072]{2,1,0:T(8,128)(2,1)} %reshape.154), calls=%async_computation.1 | async-start | bytes 7864320 | tf_op jit(solution)/shard_map/all_to_all | solution.py:106
  224.2 6.8 %reshape.159 = f32[576,24,128]{2,1,0:T(8,128)} reshape(bf16[16,36,3072]{2,1,0:T(8,128)(2,1)} %all-to-all-done.2) | data formatting | bytes 10616832 | tf_op jit(solution)/shard_map/convert_element_type | solution.py:18
  231.0 4.8 multiply_convert_fusion.2
  235.9 1.8 fusion.4
  237.7 0.9 copy-done.12
  238.6 2.7 multiply_convert_fusion.4
  241.3 66.2 %all-to-all-done.1 = bf16[16,36,3072]{2,1,0:T(8,128)(2,1)} async-done(((bf16[16,36,3072]{2,1,0:T(8,128)(2,1)}), bf16[16,36,3072]{2,1,0:T(8,128)(2,1)}, u32[]{:S(2)}, u32[]{:S(2)}) %all-to-all-start.1) | async-done | bytes 3538976 | tf_op jit(solution)/shard_map/all_to_all | solution.py:106
  307.5 5.6 reshape.160
  313.1 5.8 %multiply_reduce_fusion = f32[576]{0:T(1024)S(1)} fusion(f32[576,3072]{1,0:T(8,128)} %reshape.160, bf16[576,336]{0,1:T(8,128)(2,1)S(1)} %get-tuple-element.9, bf16[1,336,3072]{2,1,0:T(8,128)(2,1)} %param.15), kind=kOutput, calls=%fused_computation.4 | convolution fusion | flops 1192623616 | bytes 9531648 | tf_op jit(solution)/shard_map/dot_general | solution.py:30
  319.0 32.6 %psum.7 = bf16[16,36]{1,0:T(8,128)(2,1)S(1)} all-reduce(f32[16,36]{1,0:T(8,128)S(1)} %reshape_reshape.4), channel_id=1, replica_groups=mesh['dp'=16,'expert'=16] {'dp'}, use_global_device_ids=true, to_apply=%region_7.8 | all-reduce | flops 576 | bytes 3456 | tf_op jit(solution)/shard_map/psum | solution.py:126
  351.6 0.6 copy.60
  352.2 14.2 %all-to-all-start.5 = ((bf16[16,1,36]{2,1,0:T(2,128)(2,1)}), bf16[16,1,36]{2,1,0:T(2,128)(2,1)S(1)}, u32[]{:S(2)}, u32[]{:S(2)}) async-start(bf16[16,1,36]{2,1,0:T(2,128)(2,1)} %copy.60), calls=%async_computation.5 | async-start | bytes 16384 | tf_op jit(solution)/shard_map/all_to_all | solution.py:132
  366.6 9.1 %all-to-all-done.5 = bf16[16,1,36]{2,1,0:T(2,128)(2,1)S(1)} async-done(((bf16[16,1,36]{2,1,0:T(2,128)(2,1)}), bf16[16,1,36]{2,1,0:T(2,128)(2,1)S(1)}, u32[]{:S(2)}, u32[]{:S(2)}) %all-to-all-start.5) | async-done | bytes 1184 | tf_op jit(solution)/shard_map/all_to_all | solution.py:132
  375.8 0.9 select_reduce_fusion
  376.8 12.5 %all_to_all.35 = bf16[16,1,36]{2,1,0:T(2,128)(2,1)S(1)} all-to-all(bf16[16,1,36]{2,1,0:T(2,128)(2,1)S(1)} %convert_element_type.216), channel_id=1, replica_groups=mesh['dp'=16,'expert'=16] {'expert'}, dimensions={0} | all-to-all | bytes 2304 | tf_op jit(solution)/shard_map/all_to_all | solution.py:107
  389.3 5.4 multiply_convert_fusion
  394.7 4.7 convert_element_type.179
  399.4 5.1 multiply_convert_fusion.5
  404.6 2.0 fusion.11
  406.6 3.9 add_convert_fusion
  410.5 4.7 convert_element_type.191
  415.2 14.8 %copy.61 = bf16[16,36,3072]{1,0,2:T(8,128)(2,1)} copy(bf16[16,36,3072]{2,1,0:T(8,128)(2,1)} %convert_element_type.191) | data formatting | bytes 7077888
  430.0 18.1 %reshape.164 = bf16[3072,576]{1,0:T(8,128)(2,1)} reshape(bf16[3072,16,36]{2,1,0:T(8,128)(2,1)} %bitcast.88) | data formatting | bytes 7077888
  448.2 5.6 reshape.162
  453.8 2.2 mul.81
  456.0 6.3 %fusion = bf16[576,3072]{1,0:T(8,128)(2,1)} fusion(f32[576,3072]{1,0:T(8,128)} %reshape.162, f32[72,8,24,128]{3,2,1,0:T(8,128)S(1)} %bitcast.89), kind=kLoop, calls=%fused_computation.2 | loop fusion | flops 3538944 | bytes 17694720 | tf_op jit(solution)/shard_map/convert_element_type | solution.py:20
  462.4 6.3 %fusion.3 = bf16[1,336,3072]{2,1,0:T(8,128)(2,1)} fusion(bf16[576,336]{0,1:T(8,128)(2,1)S(1)} %copy-done.6, f32[576,3072]{1,0:T(8,128)} %reshape.160, f32[576]{0:T(1024)S(1)} %reshape.163), kind=kOutput, calls=%fused_computation.14 | convolution fusion | flops 1193656320 | bytes 9531648 | tf_op jit(solution)/shard_map/dot_general | solution.py:8
  468.6 54.9 %reduce-scatter.4.cloned.1.call-done = bf16[192,576]{1,0:T(8,128)(2,1)} async-done(((bf16[3072,576]{1,0:T(8,128)(2,1)}), bf16[192,576]{1,0:T(8,128)(2,1)}) %reduce-scatter.4.cloned.1.call-update) | async-done | bytes 221200
  523.5 2.1 reshape.165
  525.6 1.4 copy.62
  527.0 18.5 %all-to-all-start.4 = ((bf16[16,36,192]{2,1,0:T(8,128)(2,1)}), bf16[16,36,192]{2,1,0:T(8,128)(2,1)S(1)}, u32[]{:S(2)}, u32[]{:S(2)}) async-start(bf16[16,36,192]{2,1,0:T(8,128)(2,1)} %copy.62), calls=%async_computation.4 | async-start | bytes 655360 | tf_op jit(solution)/shard_map/all_to_all | solution.py:131
  545.5 5.3 fusion.2
  550.8 3.1 fusion.1
  553.9 3.2 all-to-all-done.4
  557.5 0.9 fusion.20
  (57 shorter events, 2.7 us)
Async XLA Ops:
  7.2 231.4 %copy-start = (bf16[1,336,3072]{2,1,0:T(8,128)(2,1)S(1)}, bf16[1,336,3072]{2,1,0:T(8,128)(2,1)}, u32[]{:S(2)}) copy-start(bf16[1,336,3072]{2,1,0:T(8,128)(2,1)} %param.14) | copy-start | bytes 6193156
  12.8 59.0 %all-to-all-start.3 = ((bf16[16,2,432]{2,1,0:T(2,128)(2,1)}), bf16[16,2,432]{2,1,0:T(2,128)(2,1)S(1)}, u32[]{:S(2)}, u32[]{:S(2)}) async-start(bf16[16,2,432]{2,1,0:T(2,128)(2,1)} %reshape.179), calls=%async_computation.3 | async-start | bytes 65536 | tf_op jit(solution)/shard_map/all_to_all | solution.py:94
  71.8 16.6 %copy-start.9 = (bf16[128,192]{0,1:T(8,128)(2,1)S(1)}, bf16[128,192]{0,1:T(8,128)(2,1)}, u32[]{:S(2)}) copy-start(bf16[128,192]{0,1:T(8,128)(2,1)} %param.12) | copy-start | bytes 147460
  71.8 140.7 %all-to-all-start.2 = ((bf16[16,36,3072]{2,1,0:T(8,128)(2,1)}), bf16[16,36,3072]{2,1,0:T(8,128)(2,1)}, u32[]{:S(2)}, u32[]{:S(2)}) async-start(bf16[16,36,3072]{2,1,0:T(8,128)(2,1)} %reshape.155), calls=%async_computation.2 | async-start | bytes 7864320 | tf_op jit(solution)/shard_map/all_to_all | solution.py:93
  212.5 95.0 %all-to-all-start.1 = ((bf16[16,36,3072]{2,1,0:T(8,128)(2,1)}), bf16[16,36,3072]{2,1,0:T(8,128)(2,1)}, u32[]{:S(2)}, u32[]{:S(2)}) async-start(bf16[16,36,3072]{2,1,0:T(8,128)(2,1)} %reshape.154), calls=%async_computation.1 | async-start | bytes 7864320 | tf_op jit(solution)/shard_map/all_to_all | solution.py:106
  231.0 4.9 copy-start.3
  237.7 0.9 copy-start.12
  241.3 71.8 %copy-start.5 = (bf16[576,336]{0,1:T(8,128)(2,1)}, bf16[576,336]{0,1:T(8,128)(2,1)S(1)}, u32[]{:S(2)}) copy-start(bf16[576,336]{0,1:T(8,128)(2,1)S(1)} %get-tuple-element.9) | copy-start | bytes 1161220
  313.1 53.4 %copy-start.11 = (bf16[128,4]{0,1:T(4,128)(2,1)S(1)}, bf16[128,4]{0,1:T(4,128)(2,1)}, u32[]{:S(2)}) copy-start(bf16[128,4]{0,1:T(4,128)(2,1)} %param.11) | copy-start | bytes 3076
  352.2 23.5 %all-to-all-start.5 = ((bf16[16,1,36]{2,1,0:T(2,128)(2,1)}), bf16[16,1,36]{2,1,0:T(2,128)(2,1)S(1)}, u32[]{:S(2)}, u32[]{:S(2)}) async-start(bf16[16,1,36]{2,1,0:T(2,128)(2,1)} %copy.60), calls=%async_computation.5 | async-start | bytes 16384 | tf_op jit(solution)/shard_map/all_to_all | solution.py:132
  366.3 157.2 %reduce-scatter.4.cloned.1.call-start = ((), (), s32[]{:S(2)}) async-start(), calls=%async_computation.7 | async-start | bytes 4177920
  399.4 5.2 copy-start.4
  404.5 2.1 copy-start.7
  456.0 6.4 %copy-start.6 = (bf16[576,336]{0,1:T(8,128)(2,1)S(1)}, bf16[576,336]{0,1:T(8,128)(2,1)}, u32[]{:S(2)}) copy-start(bf16[576,336]{0,1:T(8,128)(2,1)} %copy-done.5) | copy-start | bytes 1161220
  527.0 30.1 %all-to-all-start.4 = ((bf16[16,36,192]{2,1,0:T(8,128)(2,1)}), bf16[16,36,192]{2,1,0:T(8,128)(2,1)S(1)}, u32[]{:S(2)}, u32[]{:S(2)}) async-start(bf16[16,36,192]{2,1,0:T(8,128)(2,1)} %copy.62), calls=%async_computation.4 | async-start | bytes 655360 | tf_op jit(solution)/shard_map/all_to_all | solution.py:131
  545.5 5.3 copy-start.2
  545.5 5.3 copy-start.8
  545.5 12.9 %copy-start.1 = (bf16[1,336,3072]{2,1,0:T(8,128)(2,1)S(1)}, bf16[1,336,3072]{2,1,0:T(8,128)(2,1)}, u32[]{:S(2)}) copy-start(bf16[1,336,3072]{2,1,0:T(8,128)(2,1)} %param.14) | copy-start | bytes 6193156
  550.8 6.7 %copy-start.10 = (s32[128,24]{0,1:T(8,128)S(1)}, s32[128,24]{0,1:T(8,128)}, u32[]{:S(2)}) copy-start(s32[128,24]{0,1:T(8,128)} %param.9) | copy-start | bytes 36868
Sparse Core Ops, SparseCore 0:
  448.3 75.2 reduce-scatter.3
where the time goes:
time: 567 us; the launch traced here: 565 us
  blocking collectives  201 us (35%)
  waiting for transfers between devices  133 us (23%)
  local copies, waits for them, and re-layouts  80.3 us (14%)
  starting transfers between devices  73.1 us (13%)
  matrix products  43.8 us (8%)
  other arithmetic  19.7 us (3%)
  between operations  14.4 us (3%)
    all_gather x1, blocking collectives, on_device(): lax.all_gather(cotangent, 'dp', axis=1, tiled=True)  117 us
    all_to_all x1, waiting for transfers between devices, on_device(): lax.all_to_all(send_cot, 'expert', split_axis=0, concat_axis=0, tiled=True)  66.2 us
    unnamed x2, waiting for transfers between devices  54.9 us
    unnamed x33, local copies, waits for them, and re-layouts  39.2 us
    all_gather x1, blocking collectives, on_device(): lax.all_gather(values, 'dp', axis=1, tiled=True)  39 us
    psum x1, blocking collectives, on_device(): total_prob = lax.psum(part_prob, 'dp').astype(jnp.bfloat16)  32.6 us
    dot_general x7, matrix products, contract(): lax.dot_general(left, right, (((left_dim,), (right_dim,)), ((), ())), pre...  24.5 us
    all_to_all x1, starting transfers between devices, on_device(): lax.all_to_all(summed_rows, 'expert', split_axis=0, concat_axis=0, tiled=...  18.5 us
  transfers between devices with their start and end apart: 6, of which 4 were waited for; matrix products, arithmetic and copies ran while one was open for 11% of the time, Pallas kernels for 0%

commit v1 on v0

v1 whole, which is shorter than its diff:
```python
import functools

import jax
import jax.numpy as jnp
from jax import lax
from jax.experimental import pallas as pl
from jax.experimental.pallas import tpu as pltpu
from jax.sharding import PartitionSpec as P

MESH = pl.DeviceIdType.MESH

SLOT = 48
CAP = 36
TOK = 128
BLK = 384
ZCOL = 2 * BLK
HID = 336
HPAD = 384
FEAT = 3072
ROWS = 16 * CAP
HALF = ROWS // 2
QTR = HALF // 2


def nt(left, right):
    return lax.dot_general(left, right, (((1,), (1,)), ((), ())), preferred_element_type=jnp.float32)


def tn(left, right):
    return lax.dot_general(left, right, (((0,), (0,)), ((), ())), preferred_element_type=jnp.float32)


def nn(left, right):
    return jnp.dot(left, right, preferred_element_type=jnp.float32)


def kernel(
    mine, give, pick_w, pick, squeeze, spread, row_of, slot_of, wg, wu, wd,
    res, back, gg_out, gu_out, gd_out,
    got, sendb, recvb, xs, w2, w3, acc_gu, acc_h, hid, hidden, hid_t, hidden_t, prob, part,
    diag, dsum, ybuf, zsend, zrecv, retsend, retrecv, pbuf, py, pz, ptot, ogu, ogd,
    swap_sem, disp_send, disp_recv, w_sem, gz_send, gz_recv, gy_send, gy_recv, gd_send, gd_recv,
    rd_send, rd_recv, ro_send, ro_recv, rs_send, rs_recv, rz_send, rz_recv,
    ret_send, ret_recv, fin_sem, p_send, p_recv, pb_send, pb_recv, out_sem,
):
    d = lax.axis_index("dp")
    e = lax.axis_index("expert")
    y, zl = lax.rem(d, 4), d // 4
    par, sub = lax.rem(y, 2), y // 2
    x, zh, c = e // 4, lax.rem(e // 2, 2), lax.rem(e, 2)
    rank = zh * 8 + x * 2 + c

    def at_y(step):
        return (zl * 4 + lax.rem(y + step + 4, 4), e)

    def at_z(z):
        return (z * 4 + y, e)

    def expert_of(r):
        return lax.rem(r, 8) // 2 * 4 + r // 8 * 2 + lax.rem(r, 2)

    def remote(src, dst, ssem, rsem, dev):
        return pltpu.make_async_remote_copy(src, dst, ssem, rsem, device_id=dev, device_id_type=MESH)

    bar = pltpu.get_barrier_semaphore()
    for step in (1, 2, 3):
        pl.semaphore_signal(bar, inc=1, device_id=at_y(step), device_id_type=MESH)
        pl.semaphore_signal(bar, inc=1, device_id=at_z(lax.rem(zl + step, 4)), device_id_type=MESH)
    for step in range(1, 16):
        pl.semaphore_signal(bar, inc=1, device_id=(d, lax.rem(e + step, 16)), device_id_type=MESH)

    loads = [
        pltpu.make_async_copy(wg, w2.at[pl.ds(0, HID)], w_sem.at[0]),
        pltpu.make_async_copy(wu, w2.at[pl.ds(HPAD, HID)], w_sem.at[1]),
        pltpu.make_async_copy(wd, w3.at[pl.ds(0, HID)], w_sem.at[2]),
    ]
    for load in loads:
        load.start()
    pl.semaphore_wait(bar, 21)

    partner = (zl * 4 + y + 1 - 2 * par, e)
    swap = remote(give, got, swap_sem.at[0], swap_sem.at[1], partner)
    swap.start()
    w2[pl.ds(HID, HPAD - HID), :] = jnp.zeros((HPAD - HID, FEAT), jnp.bfloat16)
    w2[pl.ds(HPAD + HID, HPAD - HID), :] = jnp.zeros((HPAD - HID, FEAT), jnp.bfloat16)
    w3[pl.ds(HID, HPAD - HID), :] = jnp.zeros((HPAD - HID, FEAT), jnp.bfloat16)
    acc_gu[...] = jnp.zeros_like(acc_gu)
    acc_h[...] = jnp.zeros_like(acc_h)
    swap.wait()
    both = mine[...] + got[...]
    picked = nn(pick_w[...], both).astype(jnp.bfloat16)
    for r in range(16):
        sendb[r] = picked[r * SLOT : (r + 1) * SLOT]

    def dispatch(r):
        return remote(sendb.at[r], recvb.at[rank], disp_send.at[r], disp_recv.at[rank], (d, expert_of(r)))

    def arrival(r):
        return remote(sendb.at[rank], recvb.at[r], disp_send.at[rank], disp_recv.at[r], (d, expert_of(r)))

    @pl.loop(0, 16)
    def _(i):
        r = lax.rem(i + zh * 8, 16)

        @pl.when(r != rank)
        def _():
            dispatch(r).start()

    recvb[rank] = sendb[rank]

    def block(ref, z, yy, row, rows):
        return ref.at[lax.rem(yy, 2), pl.ds(pl.multiple_of(row, 16), rows),
                      pl.ds(pl.multiple_of(z * ZCOL + yy // 2 * BLK, 128), BLK)]

    def z_copy(h, j):
        ref = block(xs, zl, y, h * HALF, HALF)
        return remote(ref, ref, gz_send.at[h, j], gz_recv.at[h, j], at_z(lax.rem(zl + j, 4)))

    def z_arrival(h, j):
        ref = block(xs, lax.rem(zl - j + 4, 4), y, h * HALF, HALF)
        return remote(ref, ref, gz_send.at[h, j], gz_recv.at[h, j], at_z(lax.rem(zl + j, 4)))

    def take_half(h):
        @pl.loop(0, 8)
        def _(i):
            r = h * 8 + i

            @pl.when(r != rank)
            def _():
                arrival(r).wait_recv()

        slabs = recvb[pl.ds(h * 8, 8)].reshape(8 * SLOT, BLK)
        rows = nn(squeeze[...], slabs).astype(jnp.bfloat16)
        xs[par, pl.ds(pl.multiple_of(h * HALF, 16), HALF),
           pl.ds(pl.multiple_of(zl * ZCOL + sub * BLK, 128), BLK)] = rows
        for j in (1, 2, 3):
            z_copy(h, j).start()

    def chunk(s):
        i, j = s // 4, lax.rem(s, 4)
        h = lax.rem(zh + i, 2)
        return h, j, lax.rem(zl - j + 4, 4)

    left, right = lax.rem(y + 3, 4), lax.rem(y + 1, 4)
    across = lax.rem(y + 2, 4)

    def y_copy(s, way):
        h, j, z = chunk(s)
        ref = block(xs, z, y, h * HALF, HALF)
        return remote(ref, ref, gy_send.at[s, way], gy_recv.at[s, way], at_y(1 if way == 0 else 3))

    def y_arrival(s, way):
        h, j, z = chunk(s)
        ref = block(xs, z, left if way == 0 else right, h * HALF, HALF)
        return remote(ref, ref, gy_send.at[s, way], gy_recv.at[s, way], at_y(1 if way == 0 else 3))

    def d_copy(s, way):
        h, j, z = chunk(s)
        ref = block(xs, z, left if way == 0 else right, h * HALF + way * QTR, QTR)
        return remote(ref, ref, gd_send.at[s, way], gd_recv.at[s, way], at_y(1 if way == 0 else 3))

    def d_arrival(s, way):
        h, j, z = chunk(s)
        ref = block(xs, z, across, h * HALF + way * QTR, QTR)
        return remote(ref, ref, gd_send.at[s, way], gd_recv.at[s, way], at_y(1 if way == 0 else 3))

    take_half(zh)
    y_copy(0, 0).start()
    y_copy(0, 1).start()
    for load in loads:
        load.wait()

    @pl.loop(0, 9)
    def _(s):
        @pl.when(s == 2)
        def _():
            take_half(1 - zh)

        @pl.when(s < 7)
        def _():
            h, j, z = chunk(s + 1)

            @pl.when(j > 0)
            def _():
                z_arrival(h, j).wait_recv()

            y_copy(s + 1, 0).start()
            y_copy(s + 1, 1).start()

        @pl.when(s < 8)
        def _():
            for way in (0, 1):
                y_arrival(s, way).wait_recv()
                d_copy(s, way).start()

        @pl.when(s > 0)
        def _():
            for way in (0, 1):
                d_arrival(s - 1, way).wait_recv()
            h, j, z = chunk(s - 1)
            rows = pl.ds(pl.multiple_of(h * HALF, 16), HALF)
            cols = pl.ds(pl.multiple_of(z * ZCOL, 128), ZCOL)
            acc_gu[rows, :] += nt(xs[0, rows, cols], w2[:, cols])
            acc_h[rows, :] += nt(xs[1, rows, cols], w3[:, cols])

            @pl.when(j == 3)
            def _():
                @pl.loop(0, HALF // 32)
                def _(b):
                    part_rows = pl.ds(pl.multiple_of(h * HALF + b * 32, 16), 32)
                    gate = acc_gu[part_rows, pl.ds(0, HPAD)]
                    upper = acc_gu[part_rows, pl.ds(HPAD, HPAD)]
                    grad = acc_h[part_rows, :]
                    sig = jax.nn.sigmoid(gate)
                    swished = gate * sig
                    act = (swished * upper).astype(jnp.bfloat16)
                    hidden[part_rows, :] = act
                    hid[part_rows, pl.ds(0, HPAD)] = (
                        grad * upper * sig * (1.0 + gate * (1.0 - sig))
                    ).astype(jnp.bfloat16)
                    hid[part_rows, pl.ds(HPAD, HPAD)] = (grad * swished).astype(jnp.bfloat16)
                    total = jnp.sum(act.astype(jnp.float32) * grad, axis=1, keepdims=True)
                    prob[part_rows, :] = jnp.broadcast_to(total, (32, 128))

    for h in (0, 1):
        pbuf[pl.ds(h * 8, 8), :] = jnp.dot(
            row_of[...], prob[pl.ds(h * HALF, HALF), :] * slot_of[...],
            precision=lax.Precision.HIGHEST, preferred_element_type=jnp.float32,
        )

    def p_y(j):
        return remote(pbuf, py.at[j - 1], p_send.at[j - 1], p_recv.at[j - 1], at_y(j))

    def p_z(j):
        return remote(pz.at[3], pz.at[j - 1], p_send.at[2 + j], p_recv.at[2 + j], at_z(lax.rem(zl + j, 4)))

    def p_b(step):
        return remote(ptot, back.at[rank], pb_send.at[step], pb_recv.at[rank],
                      (d, lax.rem(e + step, 16)))

    for j in (1, 2, 3):
        p_y(j).start()

    def piece(yy, z, row, rows):
        return (pl.ds(pl.multiple_of(lax.rem(yy, 2) * HALF + row, 16), rows),
                pl.ds(pl.multiple_of(z * ZCOL + yy // 2 * BLK, 128), BLK))

    def zdest(q):
        return lax.rem(zl + 1 + q, 4)

    def diag_copy(q, way):
        src = part.at[piece(across, zdest(q), way * QTR, QTR)]
        return remote(src, diag.at[q, way], rd_send.at[q, way], rd_recv.at[q, way], at_y(1 if way == 0 else 3))

    def own_copy(q, way):
        to = right if way == 0 else left
        src = part.at[piece(to, zdest(q), (1 - way) * QTR, QTR)]
        return remote(src, ybuf.at[q, way, 1 - way], ro_send.at[q, way], ro_recv.at[q, way], at_y(1 if way == 0 else 3))

    def sum_copy(q, way):
        return remote(dsum.at[q, way], ybuf.at[q, way, way], rs_send.at[q, way], rs_recv.at[q, way],
                      at_y(1 if way == 0 else 3))

    def zred_copy(q):
        return remote(zsend.at[q], zrecv.at[q], rz_send.at[q], rz_recv.at[q], at_z(zdest(q)))

    def make_part(q):
        cols = pl.ds(pl.multiple_of(zdest(q) * ZCOL, 128), ZCOL)
        part[:, cols] = nn(hid[...], w2[:, cols]).astype(jnp.bfloat16)
        for way in (0, 1):
            diag_copy(q, way).start()
        for way in (0, 1):
            own_copy(q, way).start()

    def out_copies(q):
        cols = pl.ds(pl.multiple_of(q * ZCOL, 128), ZCOL)
        return (
            pltpu.make_async_copy(ogu.at[pl.ds(0, HID), cols], gg_out.at[:, cols], out_sem.at[q, 0]),
            pltpu.make_async_copy(ogu.at[pl.ds(HPAD, HID), cols], gu_out.at[:, cols], out_sem.at[q, 1]),
            pltpu.make_async_copy(ogd.at[pl.ds(0, HID), cols], gd_out.at[:, cols], out_sem.at[q, 2]),
        )

    def weight_grads(q):
        cols = pl.ds(pl.multiple_of(q * ZCOL, 128), ZCOL)
        ogu[:, cols] = nn(hid_t[...], xs[0, :, cols]).astype(jnp.bfloat16)
        ogd[:, cols] = nn(hidden_t[...], xs[1, :, cols]).astype(jnp.bfloat16)
        for out in out_copies(q):
            out.start()

    def y_sum(q):
        for way in (0, 1):
            own_copy(q, way).wait_recv()
            sum_copy(q, way).wait_recv()
        own = part[piece(y, zdest(q), 0, HALF)].astype(jnp.float32)
        return own + (ybuf[q, 0].reshape(HALF, BLK).astype(jnp.float32)
                      + ybuf[q, 1].reshape(HALF, BLK).astype(jnp.float32))

    make_part(0)
    hid_t[...] = hid[...].T
    hidden_t[...] = hidden[...].T

    @pl.loop(0, 4)
    def _(q):
        @pl.when(q < 3)
        def _():
            make_part(q + 1)

        for way in (0, 1):
            diag_copy(q, way).wait_recv()
            to = right if way == 0 else left
            dsum[q, way] = (
                part[piece(to, zdest(q), way * QTR, QTR)].astype(jnp.float32)
                + diag[q, way].astype(jnp.float32)
            ).astype(jnp.bfloat16)
            sum_copy(q, way).start()

        weight_grads(q)

        @pl.when(q == 0)
        def _():
            for j in (1, 2, 3):
                p_y(j).wait_recv()
            pz[3] = pbuf[...] + py[0] + py[1] + py[2]
            for j in (1, 2, 3):
                p_z(j).start()

        @pl.when(q == 1)
        def _():
            for j in (1, 2, 3):
                p_z(j).wait_recv()
            ptot[...] = pz[0] + pz[1] + pz[2] + pz[3]
            back[rank] = ptot[...]

            @pl.loop(1, 16)
            def _(step):
                p_b(step).start()

        @pl.when(q > 0)
        def _():
            zsend[q - 1] = y_sum(q - 1).astype(jnp.bfloat16)
            zred_copy(q - 1).start()

    total = y_sum(3)
    for q in range(3):
        zred_copy(q).wait_recv()
        total += zrecv[q].astype(jnp.float32)
    slabs = nn(spread[...], total.astype(jnp.bfloat16)).astype(jnp.bfloat16)
    for i in range(8):
        retsend[i] = slabs[i * SLOT : (i + 1) * SLOT]

    def ret_copy(i):
        return remote(retsend.at[i], retrecv.at[rank], ret_send.at[i], ret_recv.at[rank],
                      (d, expert_of(par * 8 + i)))

    def ret_arrival(r):
        return remote(retsend.at[0], retrecv.at[r], ret_send.at[0], ret_recv.at[r], (d, expert_of(r)))

    @pl.loop(0, 8)
    def _(i):
        @pl.when(par * 8 + i != rank)
        def _():
            ret_copy(i).start()

    fin = remote(res, res, fin_sem.at[0], fin_sem.at[1], partner)

    @pl.when(zh == par)
    def _():
        retrecv[rank] = retsend[rank - par * 8]

        @pl.loop(0, 16)
        def _(r):
            @pl.when(r != rank)
            def _():
                ret_arrival(r).wait_recv()

        res[...] = tn(pick[...], retrecv[...].reshape(16 * SLOT, BLK)).astype(jnp.bfloat16)
        fin.start()
        fin.wait_send()

    @pl.when(zh != par)
    def _():
        fin.wait_recv()

    @pl.loop(0, 16)
    def _(r):
        @pl.when(r != rank)
        def _():
            dispatch(r).wait_send()
            remote(ptot, back.at[r], pb_send.at[0], pb_recv.at[r], (d, expert_of(r))).wait_recv()

    @pl.loop(1, 16)
    def _(step):
        p_b(step).wait_send()

    @pl.loop(0, 8)
    def _(i):
        @pl.when(par * 8 + i != rank)
        def _():
            ret_copy(i).wait_send()

    @pl.loop(0, 8)
    def _(s):
        for way in (0, 1):
            y_copy(s, way).wait_send()
            d_copy(s, way).wait_send()

    for j in (1, 2, 3):
        for h in (0, 1):
            z_copy(h, j).wait_send()
        p_y(j).wait_send()
        p_z(j).wait_send()

    @pl.loop(0, 4)
    def _(q):
        for way in (0, 1):
            diag_copy(q, way).wait_send()
            own_copy(q, way).wait_send()
            sum_copy(q, way).wait_send()
        for out in out_copies(q):
            out.wait()

    for q in range(3):
        zred_copy(q).wait_send()


def on_device(values, exponents, expert_ids, route_weights, cotangent, w_gate, w_up, w_down):
    share = values.shape[1]
    d = lax.axis_index("dp")
    e = lax.axis_index("expert")
    odd = (d % 2) == 1
    blocks = exponents.shape[1]
    columns = d * share + jnp.arange(share, dtype=jnp.int32)
    block_map = ((columns // 128)[None, :] == jnp.arange(blocks, dtype=jnp.int32)[:, None]).astype(jnp.bfloat16)
    factor = jnp.dot(
        jnp.exp2(exponents.astype(jnp.float32)).astype(jnp.bfloat16), block_map,
        preferred_element_type=jnp.float32,
    )
    inputs = (values.astype(jnp.float32) * factor).astype(jnp.bfloat16)

    def placed(array):
        wide = jnp.zeros((TOK, BLK - share), jnp.bfloat16)
        return jnp.where(odd, jnp.concatenate([wide, array], 1), jnp.concatenate([array, wide], 1))

    mine = placed(jnp.where(odd, cotangent, inputs))
    give = placed(jnp.where(odd, inputs, cotangent))

    order = jnp.arange(16, dtype=jnp.int32)
    expert = order % 8 // 2 * 4 + order // 8 * 2 + order % 2
    hit = expert_ids.T[None, :, :] == expert[:, None, None]
    named = jnp.any(hit, axis=1)
    weight = jnp.sum(jnp.where(hit, route_weights.astype(jnp.float32).T[None], 0.0), axis=1)
    token = jnp.arange(TOK, dtype=jnp.int32)
    earlier = (token[:, None] < token[None, :]).astype(jnp.bfloat16)
    place = jnp.dot(named.astype(jnp.bfloat16), earlier, preferred_element_type=jnp.float32)
    chosen = named[:, None, :] & (
        place[:, None, :] == jnp.arange(SLOT, dtype=jnp.float32)[None, :, None]
    )
    pick = chosen.astype(jnp.bfloat16).reshape(16 * SLOT, TOK)
    pick_w = jnp.where(chosen, jnp.where(odd, weight, 1.0)[:, None, :], 0.0).astype(jnp.bfloat16)
    pick_w = pick_w.reshape(16 * SLOT, TOK)

    slab_row = jnp.arange(8 * SLOT, dtype=jnp.int32)
    dense_row = jnp.arange(HALF, dtype=jnp.int32)
    spread = (
        (slab_row[:, None] // SLOT == dense_row[None, :] // CAP)
        & (slab_row[:, None] % SLOT == dense_row[None, :] % CAP)
    ).astype(jnp.bfloat16)
    row_of = (jnp.arange(8, dtype=jnp.int32)[:, None] == dense_row[None, :] // CAP).astype(jnp.float32)
    slot_of = (dense_row[:, None] % CAP == jnp.arange(128, dtype=jnp.int32)[None, :]).astype(jnp.float32)

    vmem, hbm = pl.BlockSpec(memory_space=pltpu.VMEM), pl.BlockSpec(memory_space=pl.ANY)
    dma = pltpu.SemaphoreType.DMA
    bf, f32 = jnp.bfloat16, jnp.float32
    grad = jax.ShapeDtypeStruct((HID, FEAT), bf)
    res, back, gg, gu, gd = pl.pallas_call(
        kernel,
        out_shape=(
            jax.ShapeDtypeStruct((TOK, BLK), bf),
            jax.ShapeDtypeStruct((16, 16, 128), f32),
            grad, grad, grad,
        ),
        in_specs=[vmem] * 8 + [hbm] * 3,
        out_specs=(vmem, vmem, hbm, hbm, hbm),
        scratch_shapes=[
            pltpu.VMEM((TOK, BLK), bf),
            pltpu.VMEM((16, SLOT, BLK), bf),
            pltpu.VMEM((16, SLOT, BLK), bf),
            pltpu.VMEM((2, ROWS, FEAT), bf),
            pltpu.VMEM((2 * HPAD, FEAT), bf),
            pltpu.VMEM((HPAD, FEAT), bf),
            pltpu.VMEM((ROWS, 2 * HPAD), f32),
            pltpu.VMEM((ROWS, HPAD), f32),
            pltpu.VMEM((ROWS, 2 * HPAD), bf),
            pltpu.VMEM((ROWS, HPAD), bf),
            pltpu.VMEM((2 * HPAD, ROWS), bf),
            pltpu.VMEM((HPAD, ROWS), bf),
            pltpu.VMEM((ROWS, 128), f32),
            pltpu.VMEM((ROWS, FEAT), bf),
            pltpu.VMEM((4, 2, QTR, BLK), bf),
            pltpu.VMEM((4, 2, QTR, BLK), bf),
            pltpu.VMEM((4, 2, 2, QTR, BLK), bf),
            pltpu.VMEM((3, HALF, BLK), bf),
            pltpu.VMEM((3, HALF, BLK), bf),
            pltpu.VMEM((8, SLOT, BLK), bf),
            pltpu.VMEM((16, SLOT, BLK), bf),
            pltpu.VMEM((16, 128), f32),
            pltpu.VMEM((3, 16, 128), f32),
            pltpu.VMEM((4, 16, 128), f32),
            pltpu.VMEM((16, 128), f32),
            pltpu.VMEM((2 * HPAD, FEAT), bf),
            pltpu.VMEM((HPAD, FEAT), bf),
            dma((2,)), dma((16,)), dma((16,)), dma((3,)),
            dma((2, 4)), dma((2, 4)), dma((8, 2)), dma((8, 2)), dma((8, 2)), dma((8, 2)),
            dma((4, 2)), dma((4, 2)), dma((4, 2)), dma((4, 2)), dma((4, 2)), dma((4, 2)),
            dma((3,)), dma((3,)),
            dma((8,)), dma((16,)), dma((2,)), dma((6,)), dma((6,)), dma((16,)), dma((16,)),
            dma((4, 3)),
        ],
        compiler_params=pltpu.CompilerParams(
            collective_id=1, has_side_effects=True, vmem_limit_bytes=56 << 20
        ),
        name="moe_backward",
    )(mine, give, pick_w, pick, spread.T, spread, row_of, slot_of, w_gate[0], w_up[0], w_down[0])

    low = jnp.where(odd, res[:, share:], res[:, :share])
    d_values = (low.astype(f32) * factor).astype(bf)
    rank = e // 2 % 2 * 8 + e // 4 * 2 + e % 2
    own = lax.dynamic_index_in_dim(back, rank, 1, keepdims=False)
    per_expert = jnp.sum(jnp.where(chosen, own[:, :SLOT, None], 0.0), axis=1)
    per_route = jnp.sum(jnp.where(hit, per_expert[:, None, :], 0.0), axis=0).T
    d_route = (per_route / route_weights.astype(f32)).astype(bf)
    return d_values, d_route, gg[None], gu[None], gd[None]


def solution(mesh):
    in_specs = (
        P("expert", "dp"),
        P("expert", None),
        P("expert", None),
        P("expert", None),
        P("expert", "dp"),
        P("expert", "dp", None),
        P("expert", "dp", None),
        P("expert", "dp", None),
    )
    out_specs = (
        P("expert", "dp"),
        P("expert", None),
        P("expert", "dp", None),
        P("expert", "dp", None),
        P("expert", "dp", None),
    )
    return jax.shard_map(
        on_device, mesh=mesh, in_specs=in_specs, out_specs=out_specs, check_vma=False
    )
```

time: 567 us -> 176 us (0.31)
  the two profiles are of different devices: /device:TPU:1 before, /device:TPU:40 now
where the time goes in v1:
time: 176 us; the launch traced here: 174 us
  Pallas kernels  152 us (86%)
  local copies, waits for them, and re-layouts  10.2 us (6%)
  other arithmetic  9.67 us (5%)
    pallas_call x1, Pallas kernels, on_device(): pl.pallas_call(kernel, out_shape=(jax.ShapeDtypeStruct((TOK, BLK), bf), j...  152 us
    unnamed x14, local copies, waits for them, and re-layouts  9.32 us

profile of v1, /device:TPU:40, one launch (start us, length us, event | category | flops | bytes accessed | tf_op | source)
XLA Modules:
  0.0 173.7 jit_solution(18049105704689461811)
XLA Ops:
  0.7 0.8 compare_reduce_fusion
  1.5 0.7 convert_bitcast_fusion
  2.2 0.8 fusion.6
  3.0 0.1 fusion.5
  3.1 0.1 eq.143
  3.2 0.6 fusion.10.row_of
  3.8 0.9 copy.19
  4.7 0.9 copy.21
  5.6 0.9 broadcast_select_fusion
  6.5 0.8 pad_select_fusion
  7.3 0.8 fusion.4.slot_of
  8.1 0.8 fusion.pick_w
  8.9 0.8 fusion.3.pick
  9.8 0.8 and_convert_fusion.1.squeeze
  10.6 0.9 and_convert_fusion.spread
  11.5 0.0 copy-start.2
  11.5 0.0 copy-start.3
  11.5 151.9 %moe_backward.1 = (bf16[128,384]{1,0:T(8,128)(2,1)}, f32[16,16,128]{2,1,0:T(8,128)}, bf16[336,3072]{1,0:T(8,128)(2,1)}, bf16[336,3072]{1,0:T(8,128)(2,1)}, bf16[336,3072]{1,0:T(8,128)(2,1)}) custom-call(bf16[128,384]{1,0:T(8,128)(2,1)} %get-tuple-element.29.mine, bf16[128,384]{1,0:T(8,128)(2,1)} %get-tuple-element.28.give, bf16[768,128]{1,0:T(8,128)(2,1)} %fusion.pick_w, ...), custom_call_target="tpu_custom_call" | custom-call | tf_op jit(solution)/shard_map/moe_backward/pallas_call | solution.py:475
  163.4 1.0 multiply_convert_fusion
  164.4 0.7 copy.24
  165.2 0.8 constant_dynamic-slice_fusion
  166.0 0.2 select_reduce_fusion
  166.2 0.0 copy-done.2
  166.2 0.1 fusion.7
  166.3 0.0 copy-done.3
  166.3 0.6 fusion.22
  166.9 0.0 copy-start.1
  166.9 3.2 %copy.29 = bf16[1,336,3072]{2,1,0:T(8,128)(2,1)} copy(bf16[1,336,3072]{2,1,0:T(8,128)(2,1)} %bitcast.39) | data formatting | bytes 4128768
  170.0 0.0 copy-done.1
  170.0 0.0 copy-start
  170.0 1.3 copy.30
  171.3 1.0 copy-done
  172.4 1.3 copy.31
  (6 shorter events, 0.1 us)
Async XLA Ops:
  11.5 154.7 %copy-start.2 = (s32[128,4]{0,1:T(4,128)S(1)}, s32[128,4]{0,1:T(4,128)}, u32[]{:S(2)}) copy-start(s32[128,4]{0,1:T(4,128)} %param.10) | copy-start | bytes 6148
  11.5 154.8 %copy-start.3 = (bf16[128,4]{0,1:T(4,128)(2,1)S(1)}, bf16[128,4]{0,1:T(4,128)(2,1)}, u32[]{:S(2)}) copy-start(bf16[128,4]{0,1:T(4,128)(2,1)} %param.11) | copy-start | bytes 3076
  166.9 3.2 %copy-start.1 = (bf16[336,3072]{1,0:T(8,128)(2,1)S(1)}, bf16[336,3072]{1,0:T(8,128)(2,1)}, u32[]{:S(2)}) copy-start(bf16[336,3072]{1,0:T(8,128)(2,1)} %get-tuple-element.13) | copy-start | bytes 6193156
  170.0 2.3 %copy-start = (bf16[336,3072]{1,0:T(8,128)(2,1)S(1)}, bf16[336,3072]{1,0:T(8,128)(2,1)}, u32[]{:S(2)}) copy-start(bf16[336,3072]{1,0:T(8,128)(2,1)} %get-tuple-element.14) | copy-start | bytes 6193156

commit v2 on v1

v2 whole, which is shorter than its diff:
```python
import functools

import jax
import jax.numpy as jnp
from jax import lax
from jax.experimental import pallas as pl
from jax.experimental.pallas import tpu as pltpu
from jax.sharding import PartitionSpec as P

MESH = pl.DeviceIdType.MESH

SLOT = 48
CAP = 36
TOK = 128
BLK = 384
ZCOL = 2 * BLK
SHARE = 192
HID = 336
HPAD = 384
FEAT = 3072
ROWS = 16 * CAP
HALF = ROWS // 2
QTR = HALF // 2
PACK = 80
SIDE = 4 * PACK


def nt(left, right):
    return lax.dot_general(left, right, (((1,), (1,)), ((), ())), preferred_element_type=jnp.float32)


def tn(left, right):
    return lax.dot_general(left, right, (((0,), (0,)), ((), ())), preferred_element_type=jnp.float32)


def nn(left, right):
    return jnp.dot(left, right, preferred_element_type=jnp.float32)


def iota(shape, axis):
    return lax.broadcasted_iota(jnp.int32, shape, axis)


def over_cap(number):
    return (number * 1821) >> 16


def kernel(
    vt, ct, exps, ids, wts, wg, wu, wd,
    dv, droute, gg_out, gu_out, gd_out,
    inp, both, factor, pick, pick_t, pick_s, squeeze, spread, perm, row_of, slot_of, back, res, info, toks, sp,
    sendb, recvb, xs, ss, w2, w3, acc_gu, acc_h, hid, hidden, hid_t, hidden_t, prob, part,
    diag, dsum, ybuf, zsend, zrecv, retsend, retrecv, pbuf, py, pz, ptot, ogu, ogd,
    swap_sem, disp_send, disp_recv, w_sem, gz_send, gz_recv, gy_send, gy_recv, gd_send, gd_recv,
    info_send, info_recv, cy_send, cy_recv, ring_send, ring_recv, sib_send, sib_recv, sx_send, sx_recv,
    rd_send, rd_recv, ro_send, ro_recv, rs_send, rs_recv, rz_send, rz_recv,
    ret_send, ret_recv, fin_sem, p_send, p_recv, pb_send, pb_recv, out_sem,
):
    d = lax.axis_index("dp")
    e = lax.axis_index("expert")
    y, zl = lax.rem(d, 4), d // 4
    par, sub = lax.rem(y, 2), y // 2
    x, zh, c = e // 4, lax.rem(e // 2, 2), lax.rem(e, 2)
    rank = zh * 8 + c * 4 + x
    z8 = zh * 4 + zl

    def at_y(step):
        return (zl * 4 + lax.rem(y + step + 4, 4), e)

    def at_z(z):
        return (z * 4 + y, e)

    def at_ring(step):
        to = lax.rem(z8 + step + 8, 8)
        return (lax.rem(to, 4) * 4 + y, x * 4 + to // 4 * 2 + c)

    def expert_of(r):
        return lax.rem(r, 4) * 4 + r // 8 * 2 + lax.rem(r, 8) // 4

    def remote(src, dst, ssem, rsem, dev):
        return pltpu.make_async_remote_copy(src, dst, ssem, rsem, device_id=dev, device_id_type=MESH)

    bar = pltpu.get_barrier_semaphore()
    for step in (1, 2, 3):
        pl.semaphore_signal(bar, inc=1, device_id=at_y(step), device_id_type=MESH)
        pl.semaphore_signal(bar, inc=1, device_id=at_z(lax.rem(zl + step, 4)), device_id_type=MESH)
    for step in range(1, 16):
        pl.semaphore_signal(bar, inc=1, device_id=(d, lax.rem(e + step, 16)), device_id_type=MESH)

    for step in (1, 7):
        pl.semaphore_signal(bar, inc=1, device_id=at_ring(step), device_id_type=MESH)

    loads = [
        pltpu.make_async_copy(wg, w2.at[pl.ds(0, HID)], w_sem.at[0]),
        pltpu.make_async_copy(wu, w2.at[pl.ds(HPAD, HID)], w_sem.at[1]),
        pltpu.make_async_copy(wd, w3.at[pl.ds(0, HID)], w_sem.at[2]),
    ]
    for load in loads:
        load.start()

    block_of = (d * SHARE + iota((SHARE, 24), 0)) >> 7
    block_map = (block_of == iota((SHARE, 24), 1)).astype(jnp.bfloat16)
    factor[...] = nn(block_map, jnp.exp2(exps[...].astype(jnp.float32)).astype(jnp.bfloat16))
    inputs = (vt[...].astype(jnp.float32) * factor[...]).astype(jnp.bfloat16)

    order = iota((16, TOK), 0)
    expert = (order & 3) * 4 + (order >> 3) * 2 + ((order >> 2) & 1)
    wide = wts[...].astype(jnp.float32)
    named = jnp.zeros((16, TOK), jnp.float32)
    weight = jnp.zeros((16, TOK), jnp.float32)
    for k in range(4):
        hit = ids[pl.ds(k, 1), :] == expert
        named += jnp.where(hit, 1.0, 0.0)
        weight += jnp.where(hit, wide[k : k + 1, :], 0.0)
    earlier = jnp.where(iota((TOK, TOK), 0) < iota((TOK, TOK), 1), 1.0, 0.0).astype(jnp.bfloat16)
    place = nn(named.astype(jnp.bfloat16), earlier)
    place = jnp.where(named > 0.0, place, -1000.0)
    here = zh * 2 + c
    info[here, pl.ds(0, 16), :] = place
    info[here, pl.ds(16, 16), :] = weight

    partner = (zl * 4 + y + 1 - 2 * par, e)
    mine_at = pl.ds(pl.multiple_of(par * SHARE, 16), SHARE)
    other_at = pl.ds(pl.multiple_of((1 - par) * SHARE, 16), SHARE)
    inp[...] = inputs
    both[mine_at, :] = inputs
    own_lanes = pl.ds(pl.multiple_of(c * TOK, 128), TOK)
    toks[zh, pl.ds(pl.multiple_of(d * SHARE, 16), SHARE), own_lanes] = ct[...]

    def cot_copy(j):
        ref = toks.at[zh, pl.ds(pl.multiple_of(d * SHARE, 16), SHARE), own_lanes]
        return remote(ref, ref, cy_send.at[j - 1], cy_recv.at[j - 1], at_y(j))

    def info_copy(j):
        to = x * 4 + lax.rem(zh + j // 2, 2) * 2 + lax.rem(c + j, 2)
        return remote(info.at[here], info.at[here], info_send.at[j - 1], info_recv.at[j - 1], (d, to))

    pl.semaphore_wait(bar, 23)
    for j in (1, 2, 3):
        cot_copy(j).start()
    for j in (1, 2, 3):
        info_copy(j).start()
    swap = remote(inp, both.at[mine_at], swap_sem.at[0], swap_sem.at[1], partner)
    swap.start()

    slots = iota((SLOT, TOK), 0).astype(jnp.float32)
    for r in range(16):
        chosen = place[r : r + 1, :] == slots
        pick[pl.ds(r * SLOT, SLOT), :] = jnp.where(chosen, 1.0, 0.0).astype(jnp.bfloat16)
    dense = iota((QTR, 4 * SLOT), 0)
    squeeze[...] = jnp.where(
        iota((QTR, 4 * SLOT), 1) == dense + over_cap(dense) * (SLOT - CAP), 1.0, 0.0
    ).astype(jnp.bfloat16)

    def tok_block(o, half=None):
        src = lax.rem(z8 - o + 8, 8)
        low, count = (0, ZCOL) if half is None else (half * BLK, BLK)
        return toks.at[src // 4, pl.ds(pl.multiple_of(lax.rem(src, 4) * ZCOL + low, 16), count), own_lanes]

    def ring_copy(k, way):
        o = k - 1 if way == 0 else lax.rem(9 - k, 8)
        if k == 4:
            ref = tok_block(o, way)
        else:
            ref = tok_block(o)
        return remote(ref, ref, ring_send.at[way, k - 1], ring_recv.at[way, k - 1], at_ring(1 if way == 0 else 7))

    def ring_arrival(k, way):
        o = k if way == 0 else 8 - k
        if k == 4:
            ref = tok_block(o, way)
        else:
            ref = tok_block(o)
        return remote(ref, ref, ring_send.at[way, k - 1], ring_recv.at[way, k - 1], at_ring(1 if way == 0 else 7))

    def sib_copy(o):
        ref = tok_block(o)
        return remote(ref, ref, sib_send.at[o], sib_recv.at[o], (d, e + 1 - 2 * c))

    for j in (1, 2, 3):
        cot_copy(j).wait_recv()
    for way in (0, 1):
        ring_copy(1, way).start()
    sib_copy(0).start()

    swap.wait()

    @pl.when(c == par)
    def _():
        picked = nt(pick[...], both[...]).astype(jnp.bfloat16)
        for r in range(16):
            sendb[r] = picked[r * SLOT : (r + 1) * SLOT]

    def slot_at(r):
        return r // 8 * 4 + lax.rem(r, 4)

    def dispatch(r):
        return remote(sendb.at[r], recvb.at[slot_at(rank)], disp_send.at[r], disp_recv.at[rank], (d, expert_of(r)))

    def arrival(r):
        return remote(sendb.at[rank], recvb.at[slot_at(r)], disp_send.at[rank], disp_recv.at[r], (d, expert_of(r)))

    @pl.when(c == par)
    def _():
        @pl.loop(0, 16)
        def _(i):
            r = lax.rem(i + zh * 8, 16)

            @pl.when(r != rank)
            def _():
                dispatch(r).start()

        recvb[slot_at(rank)] = sendb[rank]

    for j in (1, 2, 3):
        info_copy(j).wait_recv()
    packed = iota((PACK, TOK), 0).astype(jnp.float32)
    for b in range(4):
        for to in range(4):
            row = zh * 8 + c * 4 + to
            chosen = info[b, pl.ds(row, 1), :] + float(CAP * (b % 2)) == packed
            pick_s[b // 2, pl.ds(to * PACK, PACK), pl.ds(b % 2 * TOK, TOK)] = jnp.where(
                chosen, info[b, pl.ds(row + 16, 1), :], 0.0
            ).astype(jnp.bfloat16)

    def s_rows(src, who, count):
        return pl.ds(pl.multiple_of(src // 4 * SIDE + who * PACK, 16), count)

    def s_cols(src):
        return pl.ds(pl.multiple_of(lax.rem(src, 4) * ZCOL, 128), ZCOL)

    def sx_copy(o, j):
        src = lax.rem(z8 - o + 8, 8)
        to = lax.rem(x + j, 4)
        return remote(sp.at[s_rows(src, to, PACK), s_cols(src)], ss.at[s_rows(src, x, PACK), s_cols(src)],
                      sx_send.at[o, j - 1], sx_recv.at[o, j - 1], (d, to * 4 + zh * 2 + c))

    def pick_chunk(o):
        sib_copy(o).wait_recv()
        src = lax.rem(z8 - o + 8, 8)
        sp[s_rows(src, 0, SIDE), s_cols(src)] = nt(pick_s[src // 4], toks[src // 4, s_cols(src), :]).astype(jnp.bfloat16)
        for j in (1, 3, 2):
            sx_copy(o, j).start()
        ss[s_rows(src, x, PACK), s_cols(src)] = sp[s_rows(src, x, PACK), s_cols(src)]

    def ring_step(k):
        for way in (0, 1):
            ring_arrival(k, way).wait_recv()
            if k < 4:
                ring_copy(k + 1, way).start()
        if k < 4:
            sib_copy(k).start()
            sib_copy(8 - k).start()
            pick_chunk(k)
            pick_chunk(8 - k)
        else:
            sib_copy(4).start()
            pick_chunk(4)

    def s_chunk(m):
        o = jnp.where(lax.rem(m, 2) == 1, (m + 1) // 2, lax.rem(8 - m // 2, 8))
        src = lax.rem(z8 - o + 8, 8)
        for j in (1, 2, 3):
            sx_copy(o, j).wait_recv()
        rows = s_rows(src, 0, SIDE)
        acc_h[rows, :] += nt(ss[rows, s_cols(src)], w3[:, s_cols(src)])

    pick_chunk(0)
    dense = iota((4 * SLOT, QTR), 1)
    spread[...] = jnp.where(
        iota((4 * SLOT, QTR), 0) == dense + over_cap(dense) * (SLOT - CAP), 1.0, 0.0
    ).astype(jnp.bfloat16)
    dense = iota((HALF, SIDE), 0)
    which = over_cap(dense)
    perm[...] = jnp.where(
        iota((HALF, SIDE), 1) == (which & 3) * PACK + (which >> 2) * CAP + dense - which * CAP, 1.0, 0.0
    ).astype(jnp.bfloat16)
    row_of[...] = jnp.where(over_cap(iota((8, HALF), 1)) == iota((8, HALF), 0), 1.0, 0.0)
    dense = iota((HALF, 128), 0)
    slot_of[...] = jnp.where(dense - over_cap(dense) * CAP == iota((HALF, 128), 1), 1.0, 0.0)
    for h in (0, 1):
        pick_t[h] = pick[pl.ds(h * 8 * SLOT, 8 * SLOT), :].T
    w2[pl.ds(HID, HPAD - HID), :] = jnp.zeros((HPAD - HID, FEAT), jnp.bfloat16)
    w2[pl.ds(HPAD + HID, HPAD - HID), :] = jnp.zeros((HPAD - HID, FEAT), jnp.bfloat16)
    w3[pl.ds(HID, HPAD - HID), :] = jnp.zeros((HPAD - HID, FEAT), jnp.bfloat16)
    acc_gu[...] = jnp.zeros_like(acc_gu)
    acc_h[...] = jnp.zeros_like(acc_h)

    def block(h, z, yy, lo=0, rows=QTR):
        return xs.at[pl.ds(pl.multiple_of(h * HALF + lax.rem(yy, 2) * QTR + lo, 16), rows),
                     pl.ds(pl.multiple_of(z * ZCOL + yy // 2 * BLK, 128), BLK)]

    def z_copy(h, z, way):
        ref = block(h, z, y)
        return remote(ref, ref, gz_send.at[h * 4 + z, way], gz_recv.at[h * 4 + z], at_z(zl + 1 - 2 * way))

    def z_arrival(h, z):
        ref = block(h, z, y)
        return remote(ref, ref, gz_send.at[h * 4 + z, 0], gz_recv.at[h * 4 + z], at_z(lax.rem(zl + 1, 4)))

    def z_each(h, z, what):
        @pl.when(jnp.logical_and(z <= zl, zl < 3))
        def _():
            what(z_copy(h, z, 0))

        @pl.when(jnp.logical_and(z >= zl, zl > 0))
        def _():
            what(z_copy(h, z, 1))

    def take_half(h):
        @pl.loop(0, 4)
        def _(k):
            r = h * 8 + par * 4 + k

            @pl.when(r != rank)
            def _():
                arrival(r).wait_recv()

        slabs = recvb[pl.ds(h * 4, 4)].reshape(4 * SLOT, BLK)
        xs[pl.ds(pl.multiple_of(h * HALF + par * QTR, 16), QTR),
           pl.ds(pl.multiple_of(zl * ZCOL + sub * BLK, 128), BLK)] = nn(squeeze[...], slabs).astype(jnp.bfloat16)
        z_each(h, zl, lambda copy: copy.start())

    def chunk(s):
        i, j = s // 4, lax.rem(s, 4)
        h = lax.rem(zh + i, 2)
        first, second, third = zl + 1 - 2 * (zl // 2), lax.rem(2 + 3 * zl, 5), 3 - 3 * (zl // 2)
        z = jnp.where(j == 0, zl, jnp.where(j == 1, first, jnp.where(j == 2, second, third)))
        return h, j, z

    left, right = lax.rem(y + 3, 4), lax.rem(y + 1, 4)
    across = lax.rem(y + 2, 4)

    def y_copy(s, way):
        h, j, z = chunk(s)
        ref = block(h, z, y)
        return remote(ref, ref, gy_send.at[s, way], gy_recv.at[s, way], at_y(1 if way == 0 else 3))

    def y_arrival(s, way):
        h, j, z = chunk(s)
        ref = block(h, z, left if way == 0 else right)
        return remote(ref, ref, gy_send.at[s, way], gy_recv.at[s, way], at_y(1 if way == 0 else 3))

    CUT = ((0, 80), (80, 64))

    def turn(n, way):
        return 1 + 2 * lax.rem(n + way, 2)

    def d_copy(s, way):
        h, j, z = chunk(s)
        ref = block(h, z, lax.rem(y + 4 - turn(s, way), 4), *CUT[way])
        return remote(ref, ref, gd_send.at[s, way], gd_recv.at[s, way], at_y(turn(s, way)))

    def d_arrival(s, way):
        h, j, z = chunk(s)
        ref = block(h, z, across, *CUT[way])
        return remote(ref, ref, gd_send.at[s, way], gd_recv.at[s, way], at_y(turn(s, way)))

    take_half(zh)
    y_copy(0, 0).start()
    y_copy(0, 1).start()
    for load in loads:
        load.wait()

    @pl.loop(0, 9)
    def _(s):
        @pl.when(s == 3)
        def _():
            take_half(1 - zh)

        @pl.when(s < 7)
        def _():
            h, j, z = chunk(s + 1)

            @pl.when(j > 0)
            def _():
                z_arrival(h, z).wait_recv()
                z_each(h, z, lambda copy: copy.start())

            y_copy(s + 1, 0).start()
            y_copy(s + 1, 1).start()

        @pl.when(s < 8)
        def _():
            for way in (0, 1):
                y_arrival(s, way).wait_recv()
            for way in (0, 1):
                d_copy(s, way).start()

        for k in (1, 2, 3, 4):
            @pl.when(s == k)
            def _(k=k):
                ring_step(k)

        @pl.when(s > 0)
        def _():
            for way in (0, 1):
                d_arrival(s - 1, way).wait_recv()
            h, j, z = chunk(s - 1)
            rows = pl.ds(pl.multiple_of(h * HALF, 16), HALF)
            cols = pl.ds(pl.multiple_of(z * ZCOL, 128), ZCOL)
            acc_gu[rows, :] += nt(xs[rows, cols], w2[:, cols])

            @pl.when(j == 3)
            def _():
                @pl.loop(0, HALF // 32)
                def _(b):
                    part_rows = pl.ds(pl.multiple_of(h * HALF + b * 32, 16), 32)
                    gate = acc_gu[part_rows, pl.ds(0, HPAD)]
                    upper = acc_gu[part_rows, pl.ds(HPAD, HPAD)]
                    sig = jax.nn.sigmoid(gate)
                    swished = gate * sig
                    hidden[part_rows, :] = (swished * upper).astype(jnp.bfloat16)
                    acc_gu[part_rows, pl.ds(0, HPAD)] = upper * sig * (1.0 + gate * (1.0 - sig))
                    acc_gu[part_rows, pl.ds(HPAD, HPAD)] = swished

        @pl.when(s > 2)
        def _():
            s_chunk(s - 3)

    for h in (0, 1):
        hidden_t[:, pl.ds(h * SIDE, SIDE)] = nn(hidden[pl.ds(h * HALF, HALF), :].T, perm[...]).astype(jnp.bfloat16)
    s_chunk(6)
    s_chunk(7)

    for h in (0, 1):
        grad = acc_h[pl.ds(h * SIDE, SIDE), :]
        high = grad.astype(jnp.bfloat16)
        low = (grad - high.astype(jnp.float32)).astype(jnp.bfloat16)
        acc_h[pl.ds(h * HALF, HALF), :] = nn(perm[...], high) + nn(perm[...], low)

    @pl.loop(0, ROWS // 32)
    def _(b):
        part_rows = pl.ds(pl.multiple_of(b * 32, 16), 32)
        grad = acc_h[part_rows, :]
        hid[part_rows, pl.ds(0, HPAD)] = (grad * acc_gu[part_rows, pl.ds(0, HPAD)]).astype(jnp.bfloat16)
        hid[part_rows, pl.ds(HPAD, HPAD)] = (grad * acc_gu[part_rows, pl.ds(HPAD, HPAD)]).astype(jnp.bfloat16)
        total = jnp.sum(hidden[part_rows, :].astype(jnp.float32) * grad, axis=1, keepdims=True)
        prob[part_rows, :] = jnp.broadcast_to(total, (32, 128))

    for h in (0, 1):
        pbuf[pl.ds(h * 8, 8), :] = jnp.dot(
            row_of[...], prob[pl.ds(h * HALF, HALF), :] * slot_of[...],
            precision=lax.Precision.HIGHEST, preferred_element_type=jnp.float32,
        )

    def p_y(j):
        return remote(pbuf, py.at[j - 1], p_send.at[j - 1], p_recv.at[j - 1], at_y(j))

    def p_z(j):
        return remote(pz.at[3], pz.at[j - 1], p_send.at[2 + j], p_recv.at[2 + j], at_z(lax.rem(zl + j, 4)))

    def p_b(step):
        return remote(ptot, back.at[rank], pb_send.at[step], pb_recv.at[rank],
                      (d, lax.rem(e + step, 16)))

    for j in (1, 2, 3):
        p_y(j).start()

    def rs_step(n):
        i, q = n // 4, lax.rem(n, 4)
        return lax.rem(zh + 1 + i, 2), lax.rem(zl + 1 + q, 4)

    def piece(yy, n, lo, rows):
        h, z = rs_step(n)
        return (pl.ds(pl.multiple_of(h * HALF + lax.rem(yy, 2) * QTR + lo, 16), rows),
                pl.ds(pl.multiple_of(z * ZCOL + yy // 2 * BLK, 128), BLK))

    def diag_copy(n, way):
        lo, rows = CUT[way]
        return remote(part.at[piece(across, n, lo, rows)], diag.at[n, pl.ds(lo, rows)],
                      rd_send.at[n, way], rd_recv.at[n, way], at_y(turn(n, way)))

    def own_copy(n, way):
        lo, rows = CUT[1 - way]
        to = lax.rem(y + turn(n, way), 4)
        return remote(part.at[piece(to, n, lo, rows)], ybuf.at[n, way, pl.ds(lo, rows)],
                      ro_send.at[n, way], ro_recv.at[n, way], at_y(turn(n, way)))

    def sum_copy(n, way):
        lo, rows = CUT[way]
        return remote(dsum.at[n, pl.ds(lo, rows)], ybuf.at[n, way, pl.ds(lo, rows)],
                      rs_send.at[n, way], rs_recv.at[n, way], at_y(turn(n, way)))

    def zred_copy(n):
        return remote(zsend.at[n], zrecv.at[n], rz_send.at[n], rz_recv.at[n], at_z(rs_step(n)[1]))

    def make_part(n):
        h, z = rs_step(n)
        rows = pl.ds(pl.multiple_of(h * HALF, 16), HALF)
        cols = pl.ds(pl.multiple_of(z * ZCOL, 128), ZCOL)
        part[rows, cols] = nn(hid[rows, :], w2[:, cols]).astype(jnp.bfloat16)
        for way in (0, 1):
            diag_copy(n, way).start()
        for way in (0, 1):
            own_copy(n, way).start()

    def out_copies(q):
        cols = pl.ds(pl.multiple_of(q * ZCOL, 128), ZCOL)
        return (
            pltpu.make_async_copy(ogu.at[pl.ds(0, HID), cols], gg_out.at[:, cols], out_sem.at[q, 0]),
            pltpu.make_async_copy(ogu.at[pl.ds(HPAD, HID), cols], gu_out.at[:, cols], out_sem.at[q, 1]),
            pltpu.make_async_copy(ogd.at[pl.ds(0, HID), cols], gd_out.at[:, cols], out_sem.at[q, 2]),
        )

    def weight_grads(q):
        cols = pl.ds(pl.multiple_of(q * ZCOL, 128), ZCOL)
        ogu[:, cols] = nn(hid_t[...], xs[:, cols]).astype(jnp.bfloat16)
        ogd[:, cols] = nn(hidden_t[...], ss[:, cols]).astype(jnp.bfloat16)
        for out in out_copies(q):
            out.start()

    def y_sum(n):
        for way in (0, 1):
            own_copy(n, way).wait_recv()
            sum_copy(n, way).wait_recv()
        own = part[piece(y, n, 0, QTR)].astype(jnp.float32)
        return own + (ybuf[n, 0].astype(jnp.float32) + ybuf[n, 1].astype(jnp.float32))

    def ret_rank(i, k):
        return lax.rem(zh + 1 + i, 2) * 8 + par * 4 + k

    def ret_copy(i, k):
        return remote(retsend.at[i * 4 + k], retrecv.at[rank], ret_send.at[i * 4 + k], ret_recv.at[rank],
                      (d, expert_of(ret_rank(i, k))))

    def ret_arrival(r):
        return remote(retsend.at[0], retrecv.at[r], ret_send.at[0], ret_recv.at[r], (d, expert_of(r)))

    def send_back(i):
        total = y_sum(i * 4 + 3)
        for q in range(3):
            zred_copy(i * 4 + q).wait_recv()
            total += zrecv[i * 4 + q].astype(jnp.float32)
        slabs = nn(spread[...], total.astype(jnp.bfloat16)).astype(jnp.bfloat16)
        for k in range(4):
            retsend[i * 4 + k] = slabs[k * SLOT : (k + 1) * SLOT]
            if i == 0:
                ret_copy(i, k).start()
            else:
                @pl.when(ret_rank(i, k) != rank)
                def _(k=k):
                    ret_copy(i, k).start()

                @pl.when(ret_rank(i, k) == rank)
                def _(k=k):
                    retrecv[rank] = slabs[k * SLOT : (k + 1) * SLOT]

    make_part(0)
    hid_t[...] = hid[...].T

    @pl.loop(0, 8)
    def _(n):
        @pl.when(n < 7)
        def _():
            make_part(n + 1)

        for way in (0, 1):
            diag_copy(n, way).wait_recv()
            lo, rows = CUT[way]
            to = lax.rem(y + turn(n, way), 4)
            dsum[n, pl.ds(lo, rows)] = (
                part[piece(to, n, lo, rows)].astype(jnp.float32)
                + diag[n, pl.ds(lo, rows)].astype(jnp.float32)
            ).astype(jnp.bfloat16)
            sum_copy(n, way).start()

        @pl.when(n < 4)
        def _():
            weight_grads(n)

        @pl.when(n == 1)
        def _():
            for j in (1, 2, 3):
                p_y(j).wait_recv()
            pz[3] = pbuf[...] + py[0] + py[1] + py[2]
            for j in (1, 2, 3):
                p_z(j).start()

        @pl.when(n == 3)
        def _():
            for j in (1, 2, 3):
                p_z(j).wait_recv()
            ptot[...] = pz[0] + pz[1] + pz[2] + pz[3]
            back[rank] = ptot[...]

            @pl.loop(1, 16)
            def _(step):
                p_b(step).start()

        @pl.when(jnp.logical_and(n > 0, n != 4))
        def _():
            zsend[n - 1] = y_sum(n - 1).astype(jnp.bfloat16)
            zred_copy(n - 1).start()

        @pl.when(n == 4)
        def _():
            send_back(0)

    send_back(1)

    @pl.loop(0, 16)
    def _(r):
        @pl.when(r != rank)
        def _():
            remote(ptot, back.at[r], pb_send.at[0], pb_recv.at[r], (d, expert_of(r))).wait_recv()

    own = jnp.concatenate([back[r, pl.ds(rank, 1), :] for r in range(16)], axis=0)
    own_t = jnp.concatenate([own, jnp.zeros((112, 128), jnp.float32)], axis=0).T
    per_expert = jnp.concatenate(
        [
            jnp.sum(pick[pl.ds(r * SLOT, SLOT), :].astype(jnp.float32) * own_t[:SLOT, r : r + 1],
                    axis=0, keepdims=True)
            for r in range(16)
        ],
        axis=0,
    )
    grads = [
        jnp.sum(jnp.where(ids[pl.ds(k, 1), :] == expert, per_expert, 0.0), axis=0, keepdims=True)
        for k in range(4)
    ]
    droute[...] = (jnp.concatenate(grads, axis=0) / wts[...].astype(jnp.float32)).astype(jnp.bfloat16)

    fin = remote(res.at[other_at], res.at[other_at], fin_sem.at[0], fin_sem.at[1], partner)

    @pl.when(c == par)
    def _():
        def from_half(h):
            @pl.loop(0, 8)
            def _(k):
                @pl.when(h * 8 + k != rank)
                def _():
                    ret_arrival(h * 8 + k).wait_recv()

            return nn(pick_t[h], retrecv[pl.ds(h * 8, 8)].reshape(8 * SLOT, BLK))

        total = from_half(1 - zh)
        total += from_half(zh)
        res[...] = total.T.astype(jnp.bfloat16)
        fin.start()
        fin.wait_send()

    @pl.when(c != par)
    def _():
        fin.wait_recv()

    dv[...] = (res[mine_at, :].astype(jnp.float32) * factor[...]).astype(jnp.bfloat16)

    @pl.loop(0, 16)
    def _(r):
        @pl.when(jnp.logical_and(r != rank, c == par))
        def _():
            dispatch(r).wait_send()

    for j in (1, 2, 3):
        cot_copy(j).wait_send()
        info_copy(j).wait_send()
    for k in (1, 2, 3, 4):
        for way in (0, 1):
            ring_copy(k, way).wait_send()

    @pl.loop(0, 8)
    def _(o):
        sib_copy(o).wait_send()
        for j in (1, 2, 3):
            sx_copy(o, j).wait_send()

    @pl.loop(1, 16)
    def _(step):
        p_b(step).wait_send()

    for k in range(4):
        ret_copy(0, k).wait_send()

        @pl.when(ret_rank(1, k) != rank)
        def _(k=k):
            ret_copy(1, k).wait_send()

    @pl.loop(0, 8)
    def _(s):
        for way in (0, 1):
            y_copy(s, way).wait_send()
            d_copy(s, way).wait_send()
            diag_copy(s, way).wait_send()
            own_copy(s, way).wait_send()
            sum_copy(s, way).wait_send()

    @pl.loop(0, 8)
    def _(s):
        z_each(s // 4, lax.rem(s, 4), lambda copy: copy.wait_send())

    for j in (1, 2, 3):
        p_y(j).wait_send()
        p_z(j).wait_send()

    @pl.loop(0, 4)
    def _(q):
        for out in out_copies(q):
            out.wait()

    for q in range(3):
        zred_copy(q).wait_send()
        zred_copy(4 + q).wait_send()


def finish(dv_in, droute_in, gg_in, gu_in, gd_in, dv, droute, gg, gu, gd, small, tiny, held, in_sem, out_sem):
    trips = [(dv_in, small, dv), (droute_in, tiny, droute)]
    for part in range(3):
        cols = pl.ds(part * 1024, 1024)
        for i, (src, dst) in enumerate(((gg_in, gg), (gu_in, gu), (gd_in, gd))):
            trips.append((src.at[:, cols], held.at[i, :, cols], dst.at[:, cols]))
    loads = [pltpu.make_async_copy(src, mid, in_sem.at[i]) for i, (src, mid, _) in enumerate(trips)]
    stores = [pltpu.make_async_copy(mid, dst, out_sem.at[i]) for i, (_, mid, dst) in enumerate(trips)]
    for load in loads:
        load.start()
    for load, store in zip(loads, stores):
        load.wait()
        store.start()
    for store in stores:
        store.wait()


def on_device(values, exponents, expert_ids, route_weights, cotangent, w_gate, w_up, w_down):
    vmem, hbm = pl.BlockSpec(memory_space=pltpu.VMEM), pl.BlockSpec(memory_space=pl.ANY)
    dma = pltpu.SemaphoreType.DMA
    bf, f32 = jnp.bfloat16, jnp.float32
    grad = jax.ShapeDtypeStruct((HID, FEAT), bf)
    outs = pl.pallas_call(
        kernel,
        out_shape=(
            jax.ShapeDtypeStruct((SHARE, TOK), bf),
            jax.ShapeDtypeStruct((4, TOK), bf),
            grad, grad, grad,
        ),
        in_specs=[vmem] * 5 + [hbm] * 3,
        out_specs=(vmem, vmem, hbm, hbm, hbm),
        scratch_shapes=[
            pltpu.VMEM((SHARE, TOK), bf),
            pltpu.VMEM((BLK, TOK), bf),
            pltpu.VMEM((SHARE, TOK), f32),
            pltpu.VMEM((16 * SLOT, TOK), bf),
            pltpu.VMEM((2, TOK, 8 * SLOT), bf),
            pltpu.VMEM((2, SIDE, 2 * TOK), bf),
            pltpu.VMEM((QTR, 4 * SLOT), bf),
            pltpu.VMEM((4 * SLOT, QTR), bf),
            pltpu.VMEM((HALF, SIDE), bf),
            pltpu.VMEM((8, HALF), f32),
            pltpu.VMEM((HALF, 128), f32),
            pltpu.VMEM((16, 16, 128), f32),
            pltpu.VMEM((BLK, TOK), bf),
            pltpu.VMEM((4, 32, TOK), f32),
            pltpu.VMEM((2, FEAT, 2 * TOK), bf),
            pltpu.VMEM((2 * SIDE, FEAT), bf),
            pltpu.VMEM((16, SLOT, BLK), bf),
            pltpu.VMEM((8, SLOT, BLK), bf),
            pltpu.VMEM((ROWS, FEAT), bf),
            pltpu.VMEM((2 * SIDE, FEAT), bf),
            pltpu.VMEM((2 * HPAD, FEAT), bf),
            pltpu.VMEM((HPAD, FEAT), bf),
            pltpu.VMEM((ROWS, 2 * HPAD), f32),
            pltpu.VMEM((2 * SIDE, HPAD), f32),
            pltpu.VMEM((ROWS, 2 * HPAD), bf),
            pltpu.VMEM((ROWS, HPAD), bf),
            pltpu.VMEM((2 * HPAD, ROWS), bf),
            pltpu.VMEM((HPAD, 2 * SIDE), bf),
            pltpu.VMEM((ROWS, 128), f32),
            pltpu.VMEM((ROWS, FEAT), bf),
            pltpu.VMEM((8, QTR, BLK), bf),
            pltpu.VMEM((8, QTR, BLK), bf),
            pltpu.VMEM((8, 2, QTR, BLK), bf),
            pltpu.VMEM((8, QTR, BLK), bf),
            pltpu.VMEM((8, QTR, BLK), bf),
            pltpu.VMEM((8, SLOT, BLK), bf),
            pltpu.VMEM((16, SLOT, BLK), bf),
            pltpu.VMEM((16, 128), f32),
            pltpu.VMEM((3, 16, 128), f32),
            pltpu.VMEM((4, 16, 128), f32),
            pltpu.VMEM((16, 128), f32),
            pltpu.VMEM((2 * HPAD, FEAT), bf),
            pltpu.VMEM((HPAD, FEAT), bf),
            dma((2,)), dma((16,)), dma((16,)), dma((3,)),
            dma((8, 2)), dma((8,)), dma((8, 2)), dma((8, 2)), dma((8, 2)), dma((8, 2)),
            dma((3,)), dma((3,)), dma((3,)), dma((3,)), dma((2, 4)), dma((2, 4)), dma((8,)), dma((8,)),
            dma((8, 3)), dma((8, 3)),
            dma((8, 2)), dma((8, 2)), dma((8, 2)), dma((8, 2)), dma((8, 2)), dma((8, 2)),
            dma((8,)), dma((8,)),
            dma((8,)), dma((16,)), dma((2,)), dma((6,)), dma((6,)), dma((16,)), dma((16,)),
            dma((4, 3)),
        ],
        compiler_params=pltpu.CompilerParams(
            collective_id=1, has_side_effects=True, vmem_limit_bytes=56 << 20
        ),
        name="moe_backward",
    )(values.T, cotangent.T, exponents.T, expert_ids.T, route_weights.T, w_gate[0], w_up[0], w_down[0])
    dv, droute, gg, gu, gd = pl.pallas_call(
        finish,
        out_shape=[jax.ShapeDtypeStruct(out.shape, bf) for out in outs],
        in_specs=[hbm] * 5,
        out_specs=[hbm] * 5,
        scratch_shapes=[
            pltpu.VMEM((SHARE, TOK), bf),
            pltpu.VMEM((4, TOK), bf),
            pltpu.VMEM((3, HID, FEAT), bf),
            dma((11,)), dma((11,)),
        ],
        cost_estimate=pl.CostEstimate(flops=0, bytes_accessed=12 << 20, transcendentals=0),
        name="finish",
    )(*outs)
    return dv.T, droute.T, gg[None], gu[None], gd[None]


def solution(mesh):
    in_specs = (
        P("expert", "dp"),
        P("expert", None),
        P("expert", None),
        P("expert", None),
        P("expert", "dp"),
        P("expert", "dp", None),
        P("expert", "dp", None),
        P("expert", "dp", None),
    )
    out_specs = (
        P("expert", "dp"),
        P("expert", None),
        P("expert", "dp", None),
        P("expert", "dp", None),
        P("expert", "dp", None),
    )
    return jax.shard_map(
        on_device, mesh=mesh, in_specs=in_specs, out_specs=out_specs, check_vma=False
    )
```

time: 176 us -> 141 us (0.80); the launches traced: 174 us -> 140 us
  Pallas kernels: 152 us -> 140 us
  local copies, waits for them, and re-layouts: 10.2 us -> 0 us
  other arithmetic: 9.67 us -> 0 us
    pallas_call x1 -> x2, Pallas kernels: 152 us -> 140 us  [the longest x1 134 us: on_device(): pl.pallas_call(kernel, out_shape=(jax.ShapeDtypeStruct((SHARE, TOK), bf),...]
    unnamed x14 -> x0, local copies, waits for them, and re-layouts: 9.32 us -> none
    convert_element_type x8 -> x0, other arithmetic: 6.36 us -> none  [the longest x2 1.71 us: on_device(): spread = ((slab_row[:, None] // SLOT == dense_row[None, :] // CAP) & (sla...]
where the time goes in v2:
time: 141 us; the launch traced here: 140 us
  Pallas kernels  140 us (99%)
    pallas_call x1, Pallas kernels, on_device(): pl.pallas_call(kernel, out_shape=(jax.ShapeDtypeStruct((SHARE, TOK), bf),...  134 us
    pallas_call x1, Pallas kernels, on_device(): pl.pallas_call(finish, out_shape=[jax.ShapeDtypeStruct(out.shape, bf) for...  5.53 us

profile of v2, /device:TPU:40, one launch (start us, length us, event | category | flops | bytes accessed | tf_op | source)
XLA Modules:
  0.0 140.5 jit_solution(12560794167625640045)
XLA Ops:
  0.6 134.3 %moe_backward.1 = (bf16[192,128]{1,0:T(8,128)(2,1)}, bf16[4,128]{1,0:T(4,128)(2,1)}, bf16[336,3072]{1,0:T(8,128)(2,1)}, bf16[336,3072]{1,0:T(8,128)(2,1)}, bf16[336,3072]{1,0:T(8,128)(2,1)}) custom-call(bf16[192,128]{1,0:T(8,128)(2,1)} %bitcast.16, bf16[192,128]{1,0:T(8,128)(2,1)} %bitcast.17, s32[24,128]{1,0:T(8,128)} %bitcast.18, s32[4,128]{1,0:T(4,128)} %bitcast.19, ...), custom_call_target="tpu_custom_call" | custom-call | tf_op jit(solution)/shard_map/moe_backward/pallas_call | solution.py:728
  134.9 5.5 %finish.1 = (bf16[192,128]{1,0:T(8,128)(2,1)}, bf16[4,128]{1,0:T(4,128)(2,1)}, bf16[336,3072]{1,0:T(8,128)(2,1)}, bf16[336,3072]{1,0:T(8,128)(2,1)}, bf16[336,3072]{1,0:T(8,128)(2,1)}) custom-call(bf16[192,128]{1,0:T(8,128)(2,1)} %get-tuple-element.15.dv_in, bf16[4,128]{1,0:T(4,128)(2,1)} %get-tuple-element.16.droute_in, ...), custom_call_target="tpu_custom_call" | custom-call | bytes 12582912 | tf_op jit(solution)/shard_map/finish/pallas_call | solution.py:795

commit v3 on v2

--- a/solution.py
+++ b/solution.py
@@ -49,7 +49,7 @@
     vt, ct, exps, ids, wts, wg, wu, wd,
     dv, droute, gg_out, gu_out, gd_out,
     inp, both, factor, pick, pick_t, pick_s, squeeze, spread, perm, row_of, slot_of, back, res, info, toks, sp,
-    sendb, recvb, xs, ss, w2, w3, acc_gu, acc_h, hid, hidden, hid_t, hidden_t, prob, part,
+    sendb, recvb, xs, ss, w2, w3, acc_gu, acc_h, grad_x, hid, hidden, hid_t, hidden_t, prob, part,
     diag, dsum, ybuf, zsend, zrecv, retsend, retrecv, pbuf, py, pz, ptot, ogu, ogd,
     swap_sem, disp_send, disp_recv, w_sem, gz_send, gz_recv, gy_send, gy_recv, gd_send, gd_recv,
     info_send, info_recv, cy_send, cy_recv, ring_send, ring_recv, sib_send, sib_recv, sx_send, sx_recv,
@@ -183,45 +183,15 @@
         ring_copy(1, way).start()
     sib_copy(0).start()
 
-    swap.wait()
-
-    @pl.when(c == par)
-    def _():
-        picked = nt(pick[...], both[...]).astype(jnp.bfloat16)
-        for r in range(16):
-            sendb[r] = picked[r * SLOT : (r + 1) * SLOT]
-
-    def slot_at(r):
-        return r // 8 * 4 + lax.rem(r, 4)
-
-    def dispatch(r):
-        return remote(sendb.at[r], recvb.at[slot_at(rank)], disp_send.at[r], disp_recv.at[rank], (d, expert_of(r)))
-
-    def arrival(r):
-        return remote(sendb.at[rank], recvb.at[slot_at(r)], disp_send.at[rank], disp_recv.at[r], (d, expert_of(r)))
-
-    @pl.when(c == par)
-    def _():
-        @pl.loop(0, 16)
-        def _(i):
-            r = lax.rem(i + zh * 8, 16)
-
-            @pl.when(r != rank)
-            def _():
-                dispatch(r).start()
-
-        recvb[slot_at(rank)] = sendb[rank]
-
-    for j in (1, 2, 3):
-        info_copy(j).wait_recv()
-    packed = iota((PACK, TOK), 0).astype(jnp.float32)
-    for b in range(4):
-        for to in range(4):
-            row = zh * 8 + c * 4 + to
-            chosen = info[b, pl.ds(row, 1), :] + float(CAP * (b % 2)) == packed
-            pick_s[b // 2, pl.ds(to * PACK, PACK), pl.ds(b % 2 * TOK, TOK)] = jnp.where(
-                chosen, info[b, pl.ds(row + 16, 1), :], 0.0
-            ).astype(jnp.bfloat16)
+    def make_picks(hi):
+        packed = iota((PACK, TOK), 0).astype(jnp.float32)
+        for core in range(2):
+            for to in range(4):
+                row = zh * 8 + c * 4 + to
+                chosen = info[hi * 2 + core, pl.ds(row, 1), :] + float(CAP * core) == packed
+                pick_s[hi, pl.ds(to * PACK, PACK), pl.ds(core * TOK, TOK)] = jnp.where(
+                    chosen, info[hi * 2 + core, pl.ds(row + 16, 1), :], 0.0
+                ).astype(jnp.bfloat16)
 
     def s_rows(src, who, count):
         return pl.ds(pl.multiple_of(src // 4 * SIDE + who * PACK, 16), count)
@@ -248,24 +218,59 @@
             ring_arrival(k, way).wait_recv()
             if k < 4:
                 ring_copy(k + 1, way).start()
+        sib_copy(k).start()
         if k < 4:
-            sib_copy(k).start()
             sib_copy(8 - k).start()
-            pick_chunk(k)
+        pick_chunk(k)
+        if k < 4:
             pick_chunk(8 - k)
-        else:
-            sib_copy(4).start()
-            pick_chunk(4)
+
+    def offset_of(m):
+        return jnp.where(lax.rem(m, 2) == 1, (m + 1) // 2, lax.rem(8 - m // 2, 8))
 
     def s_chunk(m):
-        o = jnp.where(lax.rem(m, 2) == 1, (m + 1) // 2, lax.rem(8 - m // 2, 8))
+        o = offset_of(m)
         src = lax.rem(z8 - o + 8, 8)
         for j in (1, 2, 3):
             sx_copy(o, j).wait_recv()
         rows = s_rows(src, 0, SIDE)
         acc_h[rows, :] += nt(ss[rows, s_cols(src)], w3[:, s_cols(src)])
 
+    swap.wait()
+
+    @pl.when(c == par)
+    def _():
+        picked = nt(pick[...], both[...]).astype(jnp.bfloat16)
+        for r in range(16):
+            sendb[r] = picked[r * SLOT : (r + 1) * SLOT]
+
+    def slot_at(r):
+        return r // 8 * 4 + lax.rem(r, 4)
+
+    def dispatch(r):
+        return remote(sendb.at[r], recvb.at[slot_at(rank)], disp_send.at[r], disp_recv.at[rank], (d, expert_of(r)))
+
+    def arrival(r):
+        return remote(sendb.at[rank], recvb.at[slot_at(r)], disp_send.at[rank], disp_recv.at[r], (d, expert_of(r)))
+
+    @pl.when(c == par)
+    def _():
+        @pl.loop(0, 16)
+        def _(i):
+            r = lax.rem(i + 8 + zh * 8, 16)
+
+            @pl.when(r != rank)
+            def _():
+                dispatch(r).start()
+
+        recvb[slot_at(rank)] = sendb[rank]
+
+    info_copy(1).wait_recv()
+    make_picks(zh)
     pick_chunk(0)
+    for j in (2, 3):
+        info_copy(j).wait_recv()
+    make_picks(1 - zh)
     dense = iota((4 * SLOT, QTR), 1)
     spread[...] = jnp.where(
         iota((4 * SLOT, QTR), 0) == dense + over_cap(dense) * (SLOT - CAP), 1.0, 0.0
@@ -356,29 +361,33 @@
         ref = block(h, z, across, *CUT[way])
         return remote(ref, ref, gd_send.at[s, way], gd_recv.at[s, way], at_y(turn(s, way)))
 
+    def spread_chunk(s):
+        h, j, z = chunk(s)
+
+        @pl.when(j > 0)
+        def _():
+            z_arrival(h, z).wait_recv()
+            z_each(h, z, lambda copy: copy.start())
+
+        y_copy(s, 0).start()
+        y_copy(s, 1).start()
+
     take_half(zh)
-    y_copy(0, 0).start()
-    y_copy(0, 1).start()
+    spread_chunk(0)
+    ring_step(1)
+    spread_chunk(1)
     for load in loads:
         load.wait()
 
     @pl.loop(0, 9)
     def _(s):
-        @pl.when(s == 3)
+        @pl.when(s == 2)
         def _():
             take_half(1 - zh)
 
-        @pl.when(s < 7)
-        def _():
-            h, j, z = chunk(s + 1)
-
-            @pl.when(j > 0)
-            def _():
-                z_arrival(h, z).wait_recv()
-                z_each(h, z, lambda copy: copy.start())
-
-            y_copy(s + 1, 0).start()
-            y_copy(s + 1, 1).start()
+        @pl.when(s < 6)
+        def _():
+            spread_chunk(s + 2)
 
         @pl.when(s < 8)
         def _():
@@ -387,10 +396,11 @@
             for way in (0, 1):
                 d_copy(s, way).start()
 
-        for k in (1, 2, 3, 4):
-            @pl.when(s == k)
+        for k in (2, 3, 4):
+            @pl.when(s == k - 2)
             def _(k=k):
                 ring_step(k)
+
 
         @pl.when(s > 0)
         def _():
@@ -423,26 +433,20 @@
     s_chunk(6)
     s_chunk(7)
 
-    for h in (0, 1):
-        grad = acc_h[pl.ds(h * SIDE, SIDE), :]
+    def finish_half(h):
+        grad = acc_h[pl.ds(pl.multiple_of(h * SIDE, 16), SIDE), :]
         high = grad.astype(jnp.bfloat16)
         low = (grad - high.astype(jnp.float32)).astype(jnp.bfloat16)
-        acc_h[pl.ds(h * HALF, HALF), :] = nn(perm[...], high) + nn(perm[...], low)
-
-    @pl.loop(0, ROWS // 32)
-    def _(b):
-        part_rows = pl.ds(pl.multiple_of(b * 32, 16), 32)
-        grad = acc_h[part_rows, :]
-        hid[part_rows, pl.ds(0, HPAD)] = (grad * acc_gu[part_rows, pl.ds(0, HPAD)]).astype(jnp.bfloat16)
-        hid[part_rows, pl.ds(HPAD, HPAD)] = (grad * acc_gu[part_rows, pl.ds(HPAD, HPAD)]).astype(jnp.bfloat16)
-        total = jnp.sum(hidden[part_rows, :].astype(jnp.float32) * grad, axis=1, keepdims=True)
-        prob[part_rows, :] = jnp.broadcast_to(total, (32, 128))
-
-    for h in (0, 1):
-        pbuf[pl.ds(h * 8, 8), :] = jnp.dot(
-            row_of[...], prob[pl.ds(h * HALF, HALF), :] * slot_of[...],
-            precision=lax.Precision.HIGHEST, preferred_element_type=jnp.float32,
-        )
+        grad_x[...] = nn(perm[...], high) + nn(perm[...], low)
+
+        @pl.loop(0, HALF // 32)
+        def _(b):
+            part_rows = pl.ds(pl.multiple_of(h * HALF + b * 32, 16), 32)
+            grad = grad_x[pl.ds(pl.multiple_of(b * 32, 16), 32), :]
+            hid[part_rows, pl.ds(0, HPAD)] = (grad * acc_gu[part_rows, pl.ds(0, HPAD)]).astype(jnp.bfloat16)
+            hid[part_rows, pl.ds(HPAD, HPAD)] = (grad * acc_gu[part_rows, pl.ds(HPAD, HPAD)]).astype(jnp.bfloat16)
+            total = jnp.sum(hidden[part_rows, :].astype(jnp.float32) * grad, axis=1, keepdims=True)
+            prob[part_rows, :] = jnp.broadcast_to(total, (32, 128))
 
     def p_y(j):
         return remote(pbuf, py.at[j - 1], p_send.at[j - 1], p_recv.at[j - 1], at_y(j))
@@ -453,9 +457,6 @@
     def p_b(step):
         return remote(ptot, back.at[rank], pb_send.at[step], pb_recv.at[rank],
                       (d, lax.rem(e + step, 16)))
-
-    for j in (1, 2, 3):
-        p_y(j).start()
 
     def rs_step(n):
         i, q = n // 4, lax.rem(n, 4)
@@ -546,14 +547,25 @@
                 def _(k=k):
                     retrecv[rank] = slabs[k * SLOT : (k + 1) * SLOT]
 
+    finish_half(1 - zh)
     make_part(0)
+    make_part(1)
+    finish_half(zh)
+    for h in (0, 1):
+        pbuf[pl.ds(h * 8, 8), :] = jnp.dot(
+            row_of[...], prob[pl.ds(h * HALF, HALF), :] * slot_of[...],
+            precision=lax.Precision.HIGHEST, preferred_element_type=jnp.float32,
+        )
+
+    for j in (1, 2, 3):
+        p_y(j).start()
     hid_t[...] = hid[...].T
 
     @pl.loop(0, 8)
     def _(n):
-        @pl.when(n < 7)
-        def _():
-            make_part(n + 1)
+        @pl.when(n < 6)
+        def _():
+            make_part(n + 2)
 
         for way in (0, 1):
             diag_copy(n, way).wait_recv()
@@ -705,10 +717,10 @@
 
 def finish(dv_in, droute_in, gg_in, gu_in, gd_in, dv, droute, gg, gu, gd, small, tiny, held, in_sem, out_sem):
     trips = [(dv_in, small, dv), (droute_in, tiny, droute)]
-    for part in range(3):
-        cols = pl.ds(part * 1024, 1024)
-        for i, (src, dst) in enumerate(((gg_in, gg), (gu_in, gu), (gd_in, gd))):
-            trips.append((src.at[:, cols], held.at[i, :, cols], dst.at[:, cols]))
+    for i, (src, dst) in enumerate(((gg_in, gg), (gu_in, gu), (gd_in, gd))):
+        for part in range(3):
+            rows = pl.ds(part * 112, 112)
+            trips.append((src.at[rows], held.at[i, rows], dst.at[rows]))
     loads = [pltpu.make_async_copy(src, mid, in_sem.at[i]) for i, (src, mid, _) in enumerate(trips)]
     stores = [pltpu.make_async_copy(mid, dst, out_sem.at[i]) for i, (_, mid, dst) in enumerate(trips)]
     for load in loads:
@@ -759,6 +771,7 @@
             pltpu.VMEM((HPAD, FEAT), bf),
             pltpu.VMEM((ROWS, 2 * HPAD), f32),
             pltpu.VMEM((2 * SIDE, HPAD), f32),
+            pltpu.VMEM((HALF, HPAD), f32),
             pltpu.VMEM((ROWS, 2 * HPAD), bf),
             pltpu.VMEM((ROWS, HPAD), bf),
             pltpu.VMEM((2 * HPAD, ROWS), bf),

time: 141 us -> 135 us (0.957)
  Pallas kernels: 140 us -> 133 us
    pallas_call x1, Pallas kernels: 134 us -> 127 us  [on_device(): pl.pallas_call(kernel, out_shape=(jax.ShapeDtypeStruct((SHARE, TOK), bf),...]
where the time goes in v3:
time: 135 us; the launch traced here: 134 us
  Pallas kernels  133 us (99%)
    pallas_call x1, Pallas kernels, on_device(): pl.pallas_call(kernel, out_shape=(jax.ShapeDtypeStruct((SHARE, TOK), bf),...  127 us
    pallas_call x1, Pallas kernels, on_device(): pl.pallas_call(finish, out_shape=[jax.ShapeDtypeStruct(out.shape, bf) for...  5.58 us

profile of v3, /device:TPU:40, one launch (start us, length us, event | category | flops | bytes accessed | tf_op | source)
XLA Modules:
  0.0 133.6 jit_solution(14607723500946672093)
XLA Ops:
  0.6 127.4 %moe_backward.1 = (bf16[192,128]{1,0:T(8,128)(2,1)}, bf16[4,128]{1,0:T(4,128)(2,1)}, bf16[336,3072]{1,0:T(8,128)(2,1)}, bf16[336,3072]{1,0:T(8,128)(2,1)}, bf16[336,3072]{1,0:T(8,128)(2,1)}) custom-call(bf16[192,128]{1,0:T(8,128)(2,1)} %bitcast.16, bf16[192,128]{1,0:T(8,128)(2,1)} %bitcast.17, s32[24,128]{1,0:T(8,128)} %bitcast.18, s32[4,128]{1,0:T(4,128)} %bitcast.19, ...), custom_call_target="tpu_custom_call" | custom-call | tf_op jit(solution)/shard_map/moe_backward/pallas_call | solution.py:740
  128.0 5.6 %finish.1 = (bf16[192,128]{1,0:T(8,128)(2,1)}, bf16[4,128]{1,0:T(4,128)(2,1)}, bf16[336,3072]{1,0:T(8,128)(2,1)}, bf16[336,3072]{1,0:T(8,128)(2,1)}, bf16[336,3072]{1,0:T(8,128)(2,1)}) custom-call(bf16[192,128]{1,0:T(8,128)(2,1)} %get-tuple-element.15.dv_in, bf16[4,128]{1,0:T(4,128)(2,1)} %get-tuple-element.16.droute_in, ...), custom_call_target="tpu_custom_call" | custom-call | bytes 12582912 | tf_op jit(solution)/shard_map/finish/pallas_call | solution.py:808

commit v4 on v3

--- a/solution.py
+++ b/solution.py
@@ -13,6 +13,7 @@
 CAP = 36
 TOK = 128
 BLK = 384
+WIDE = 256
 ZCOL = 2 * BLK
 SHARE = 192
 HID = 336
@@ -54,7 +55,7 @@
     swap_sem, disp_send, disp_recv, w_sem, gz_send, gz_recv, gy_send, gy_recv, gd_send, gd_recv,
     info_send, info_recv, cy_send, cy_recv, ring_send, ring_recv, sib_send, sib_recv, sx_send, sx_recv,
     rd_send, rd_recv, ro_send, ro_recv, rs_send, rs_recv, rz_send, rz_recv,
-    ret_send, ret_recv, fin_sem, p_send, p_recv, pb_send, pb_recv, out_sem,
+    ret_send, ret_recv, p_send, p_recv, pb_send, pb_recv, out_sem,
 ):
     d = lax.axis_index("dp")
     e = lax.axis_index("expert")
@@ -89,6 +90,11 @@
 
     for step in (1, 7):
         pl.semaphore_signal(bar, inc=1, device_id=at_ring(step), device_id_type=MESH)
+
+    @pl.when(c != par)
+    def _():
+        for to in range(16):
+            pl.semaphore_signal(bar, inc=1, device_id=(d + 1 - 2 * par, to), device_id_type=MESH)
 
     loads = [
         pltpu.make_async_copy(wg, w2.at[pl.ds(0, HID)], w_sem.at[0]),
@@ -121,7 +127,6 @@
 
     partner = (zl * 4 + y + 1 - 2 * par, e)
     mine_at = pl.ds(pl.multiple_of(par * SHARE, 16), SHARE)
-    other_at = pl.ds(pl.multiple_of((1 - par) * SHARE, 16), SHARE)
     inp[...] = inputs
     both[mine_at, :] = inputs
     own_lanes = pl.ds(pl.multiple_of(c * TOK, 128), TOK)
@@ -135,7 +140,7 @@
         to = x * 4 + lax.rem(zh + j // 2, 2) * 2 + lax.rem(c + j, 2)
         return remote(info.at[here], info.at[here], info_send.at[j - 1], info_recv.at[j - 1], (d, to))
 
-    pl.semaphore_wait(bar, 23)
+    pl.semaphore_wait(bar, 31)
     for j in (1, 2, 3):
         cot_copy(j).start()
     for j in (1, 2, 3):
@@ -374,8 +379,8 @@
 
     take_half(zh)
     spread_chunk(0)
+    spread_chunk(1)
     ring_step(1)
-    spread_chunk(1)
     for load in loads:
         load.wait()
 
@@ -521,12 +526,24 @@
     def ret_rank(i, k):
         return lax.rem(zh + 1 + i, 2) * 8 + par * 4 + k
 
-    def ret_copy(i, k):
-        return remote(retsend.at[i * 4 + k], retrecv.at[rank], ret_send.at[i * 4 + k], ret_recv.at[rank],
-                      (d, expert_of(ret_rank(i, k))))
+    def ret_copy(i, k, member):
+        return remote(retsend.at[i * 4 + k, :, pl.ds(member * 128, WIDE)], retrecv.at[rank],
+                      ret_send.at[i * 4 + k, member], ret_recv.at[rank],
+                      (d - par + member, expert_of(ret_rank(i, k))))
 
     def ret_arrival(r):
-        return remote(retsend.at[0], retrecv.at[r], ret_send.at[0], ret_recv.at[r], (d, expert_of(r)))
+        return remote(retsend.at[0, :, pl.ds(0, WIDE)], retrecv.at[r], ret_send.at[0, 0], ret_recv.at[r],
+                      (d, expert_of(r)))
+
+    def ret_each(i, what):
+        for k in range(4):
+            for member in (0, 1):
+                if i == 0:
+                    what(ret_copy(i, k, member))
+                else:
+                    @pl.when(jnp.logical_or(ret_rank(i, k) != rank, par != member))
+                    def _(k=k, member=member):
+                        what(ret_copy(i, k, member))
 
     def send_back(i):
         total = y_sum(i * 4 + 3)
@@ -536,16 +553,13 @@
         slabs = nn(spread[...], total.astype(jnp.bfloat16)).astype(jnp.bfloat16)
         for k in range(4):
             retsend[i * 4 + k] = slabs[k * SLOT : (k + 1) * SLOT]
-            if i == 0:
-                ret_copy(i, k).start()
-            else:
-                @pl.when(ret_rank(i, k) != rank)
-                def _(k=k):
-                    ret_copy(i, k).start()
-
-                @pl.when(ret_rank(i, k) == rank)
-                def _(k=k):
-                    retrecv[rank] = slabs[k * SLOT : (k + 1) * SLOT]
+        ret_each(i, lambda copy: copy.start())
+        if i == 1:
+            for k in range(4):
+                for member in (0, 1):
+                    @pl.when(jnp.logical_and(ret_rank(i, k) == rank, par == member))
+                    def _(k=k, member=member):
+                        retrecv[rank] = slabs[k * SLOT : (k + 1) * SLOT, member * 128 : member * 128 + WIDE]
 
     finish_half(1 - zh)
     make_part(0)
@@ -633,30 +647,19 @@
     ]
     droute[...] = (jnp.concatenate(grads, axis=0) / wts[...].astype(jnp.float32)).astype(jnp.bfloat16)
 
-    fin = remote(res.at[other_at], res.at[other_at], fin_sem.at[0], fin_sem.at[1], partner)
-
-    @pl.when(c == par)
-    def _():
-        def from_half(h):
-            @pl.loop(0, 8)
-            def _(k):
-                @pl.when(h * 8 + k != rank)
-                def _():
-                    ret_arrival(h * 8 + k).wait_recv()
-
-            return nn(pick_t[h], retrecv[pl.ds(h * 8, 8)].reshape(8 * SLOT, BLK))
-
-        total = from_half(1 - zh)
-        total += from_half(zh)
-        res[...] = total.T.astype(jnp.bfloat16)
-        fin.start()
-        fin.wait_send()
-
-    @pl.when(c != par)
-    def _():
-        fin.wait_recv()
-
-    dv[...] = (res[mine_at, :].astype(jnp.float32) * factor[...]).astype(jnp.bfloat16)
+    def from_half(h):
+        @pl.loop(0, 8)
+        def _(k):
+            @pl.when(jnp.logical_or(h * 8 + k != rank, c != par))
+            def _():
+                ret_arrival(h * 8 + k).wait_recv()
+
+        return nn(pick_t[h], retrecv[pl.ds(h * 8, 8)].reshape(8 * SLOT, WIDE))
+
+    total = from_half(1 - zh)
+    total += from_half(zh)
+    res[...] = total.T
+    dv[...] = (res[pl.ds(pl.multiple_of(par * (WIDE - SHARE), 16), SHARE), :] * factor[...]).astype(jnp.bfloat16)
 
     @pl.loop(0, 16)
     def _(r):
@@ -681,12 +684,8 @@
     def _(step):
         p_b(step).wait_send()
 
-    for k in range(4):
-        ret_copy(0, k).wait_send()
-
-        @pl.when(ret_rank(1, k) != rank)
-        def _(k=k):
-            ret_copy(1, k).wait_send()
+    for i in (0, 1):
+        ret_each(i, lambda copy: copy.wait_send())
 
     @pl.loop(0, 8)
     def _(s):
@@ -759,7 +758,7 @@
             pltpu.VMEM((8, HALF), f32),
             pltpu.VMEM((HALF, 128), f32),
             pltpu.VMEM((16, 16, 128), f32),
-            pltpu.VMEM((BLK, TOK), bf),
+            pltpu.VMEM((WIDE, TOK), f32),
             pltpu.VMEM((4, 32, TOK), f32),
             pltpu.VMEM((2, FEAT, 2 * TOK), bf),
             pltpu.VMEM((2 * SIDE, FEAT), bf),
@@ -784,7 +783,7 @@
             pltpu.VMEM((8, QTR, BLK), bf),
             pltpu.VMEM((8, QTR, BLK), bf),
             pltpu.VMEM((8, SLOT, BLK), bf),
-            pltpu.VMEM((16, SLOT, BLK), bf),
+            pltpu.VMEM((16, SLOT, WIDE), bf),
             pltpu.VMEM((16, 128), f32),
             pltpu.VMEM((3, 16, 128), f32),
             pltpu.VMEM((4, 16, 128), f32),
@@ -797,7 +796,7 @@
             dma((8, 3)), dma((8, 3)),
             dma((8, 2)), dma((8, 2)), dma((8, 2)), dma((8, 2)), dma((8, 2)), dma((8, 2)),
             dma((8,)), dma((8,)),
-            dma((8,)), dma((16,)), dma((2,)), dma((6,)), dma((6,)), dma((16,)), dma((16,)),
+            dma((8, 2)), dma((16,)), dma((6,)), dma((6,)), dma((16,)), dma((16,)),
             dma((4, 3)),
         ],
         compiler_params=pltpu.CompilerParams(

time: 135 us -> 140 us (1.037)
  Pallas kernels: 133 us -> 139 us
    pallas_call x1, Pallas kernels: 127 us -> 134 us  [on_device(): pl.pallas_call(kernel, out_shape=(jax.ShapeDtypeStruct((SHARE, TOK), bf),...]
where the time goes in v4:
time: 140 us
  Pallas kernels  139 us (99%)
    pallas_call x1, Pallas kernels, on_device(): pl.pallas_call(kernel, out_shape=(jax.ShapeDtypeStruct((SHARE, TOK), bf),...  134 us
    pallas_call x1, Pallas kernels, on_device(): pl.pallas_call(finish, out_shape=[jax.ShapeDtypeStruct(out.shape, bf) for...  5.58 us

profile of v4, /device:TPU:40, one launch (start us, length us, event | category | flops | bytes accessed | tf_op | source)
XLA Modules:
  0.0 140.0 jit_solution(9768498785256231388)
XLA Ops:
  0.6 133.8 %moe_backward.1 = (bf16[192,128]{1,0:T(8,128)(2,1)}, bf16[4,128]{1,0:T(4,128)(2,1)}, bf16[336,3072]{1,0:T(8,128)(2,1)}, bf16[336,3072]{1,0:T(8,128)(2,1)}, bf16[336,3072]{1,0:T(8,128)(2,1)}) custom-call(bf16[192,128]{1,0:T(8,128)(2,1)} %bitcast.16, bf16[192,128]{1,0:T(8,128)(2,1)} %bitcast.17, s32[24,128]{1,0:T(8,128)} %bitcast.18, s32[4,128]{1,0:T(4,128)} %bitcast.19, ...), custom_call_target="tpu_custom_call" | custom-call | tf_op jit(solution)/shard_map/moe_backward/pallas_call | solution.py:739
  134.4 5.6 %finish.1 = (bf16[192,128]{1,0:T(8,128)(2,1)}, bf16[4,128]{1,0:T(4,128)(2,1)}, bf16[336,3072]{1,0:T(8,128)(2,1)}, bf16[336,3072]{1,0:T(8,128)(2,1)}, bf16[336,3072]{1,0:T(8,128)(2,1)}) custom-call(bf16[192,128]{1,0:T(8,128)(2,1)} %get-tuple-element.15.dv_in, bf16[4,128]{1,0:T(4,128)(2,1)} %get-tuple-element.16.droute_in, ...), custom_call_target="tpu_custom_call" | custom-call | bytes 12582912 | tf_op jit(solution)/shard_map/finish/pallas_call | solution.py:807
